TPU v7x, 512 devices: a whole 4x8x8 slice. The times are simulated.
512 devices in a mesh: dp: 64 (over y, z), emb: 8 (over x, core).
Axes of the slice: x: 4, y: 8, z: 8, core: 2. Of those that a mesh axis runs over, the one named last changes fastest.
Arguments:
- actions: bfloat16 [1024, 64, 64], P(('dp', 'emb')), may hold values from -6 to 6
- noise: bfloat16 [1024, 64, 64], P(('dp', 'emb')), may hold values from -6 to 6
- emb_ids: int32 [1024], P(('dp', 'emb')), may hold values from 0 to 23, as said below
- lengths: int32 [1024], P(('dp', 'emb')), may hold values from 16 to 64
- t_index: int32 [1024], P(('dp', 'emb')), may hold values from 0 to 999
- act_dims: int32 [24], replicated, may hold values from 7 to 56
- features: bfloat16 [1024, 8, 5120], P('dp', None, 'emb'), may hold values from -6 to 6
- enc_w: bfloat16 [24, 64, 1536], P('emb'), may hold values from -0.75 to 0.75
- dec_w: bfloat16 [24, 1536, 64], P('emb'), may hold values from -0.15625 to 0.15625
- wq: bfloat16 [1536, 1536], P('dp', 'emb'), may hold values from -0.15625 to 0.15625
- wk: bfloat16 [5120, 1536], P('dp', 'emb'), may hold values from -0.078125 to 0.078125
- wv: bfloat16 [5120, 1536], P('dp', 'emb'), may hold values from -0.078125 to 0.078125
- wo_t: bfloat16 [1536, 1536], P('dp', 'emb'), may hold values from -0.15625 to 0.15625
Outputs:
- d_wq_t: float32 [1536, 1536], P('emb')
- d_wo: float32 [1536, 1536], P('emb')
- loss: float32 [1024], P(('dp', 'emb'))
Inputs may be any that keep to these rules, and one draw needn't show every extreme that they name: `emb_ids`: embodiment i belongs to owner i // 3, the index of emb that holds its projectors. Among the 2 spans of one device at most 1 belong to one owner, and in every group of devices along emb some owner gets exactly 1 span from each device of the group.
All inputs are finite; a program needn't handle non-finite values.
Results may differ from a plain program's by a relative error of at most 0.0087.
Values may be sent and summed in bfloat16 or wider, within the bound.
A program may use at most 64 MiB of HBM per device.

v0:
```python
import math

import jax
import jax.numpy as jnp
from jax import lax
from jax.sharding import PartitionSpec as P

HD = 48
EMB_DEV = 3
TSTEPS = 1000


def step_embedding(step_values, width):
    half = width // 2
    freq = jnp.exp(-math.log(10000.0) * jnp.arange(half, dtype=jnp.float32) / half)
    angle = step_values.astype(jnp.float32)[:, None] * freq[None, :]
    return jnp.concatenate([jnp.sin(angle), jnp.cos(angle)], axis=1)


def noisy_parts(actions, noise, levels):
    fraction = (levels.astype(jnp.float32) / TSTEPS)[:, None, None]
    mixed = (1.0 - fraction) * noise.astype(jnp.float32) + fraction * actions.astype(jnp.float32)
    return mixed.astype(jnp.bfloat16)


def body(
    actions, noise, emb_ids, lengths, t_index, act_dims, features, enc_w, dec_w, wq, wk, wv, wo_t
):
    hidden_width = enc_w.shape[2]
    steps_len = actions.shape[1]
    action_width = actions.shape[2]
    per_device = actions.shape[0]
    owners = lax.axis_size("emb")
    group = per_device * owners
    rows_group = group * steps_len
    position = lax.axis_index("emb")
    scale = 1.0 / math.sqrt(HD)
    query_weight, key_weight, value_weight, out_weight = (
        lax.all_gather(wq, "dp", axis=0, tiled=True),
        lax.all_gather(wk, "dp", axis=0, tiled=True),
        lax.all_gather(wv, "dp", axis=0, tiled=True),
        lax.all_gather(wo_t, "dp", axis=0, tiled=True),
    )
    columns = query_weight.shape[1]
    heads_here = columns // HD
    ids_group, length_group, level_group = (
        lax.all_gather(emb_ids, "emb", axis=0, tiled=True),
        lax.all_gather(lengths, "emb", axis=0, tiled=True),
        lax.all_gather(t_index, "emb", axis=0, tiled=True),
    )
    context_len = features.shape[1]
    piece = lax.all_gather(features, "emb", axis=2, tiled=True)
    width = piece.shape[2]
    flat_piece = piece.reshape(group * context_len, width)
    key_acc = jnp.dot(flat_piece, key_weight, preferred_element_type=jnp.float32)
    value_acc = jnp.dot(flat_piece, value_weight, preferred_element_type=jnp.float32)
    dec_group, act_group, noise_group = (
        lax.all_gather(dec_w, "emb", axis=0, tiled=True),
        lax.all_gather(actions, "emb", axis=0, tiled=True),
        lax.all_gather(noise, "emb", axis=0, tiled=True),
    )
    noisy_own = noisy_parts(actions, noise, t_index)
    owner_of = emb_ids // EMB_DEV
    local_of = emb_ids % EMB_DEV
    earlier = jnp.arange(per_device)[None, :] < jnp.arange(per_device)[:, None]
    same_owner = owner_of[None, :] == owner_of[:, None]
    slot_of = jnp.sum((earlier & same_owner).astype(jnp.int32), axis=1)
    slot_count = (per_device + owners - 1) // owners
    target = (
        (owner_of[:, None, None] == jnp.arange(owners)[None, :, None])
        & (slot_of[:, None, None] == jnp.arange(slot_count)[None, None, :])
    ).astype(jnp.bfloat16)
    send_rows = jnp.einsum(
        "cos,cxa->osxa", target, noisy_own, preferred_element_type=jnp.float32
    ).astype(jnp.bfloat16)
    chooser = (local_of[:, None] == jnp.arange(EMB_DEV)[None, :]).astype(jnp.bfloat16)
    send_pick = jnp.einsum("cos,cj->osj", target, chooser, preferred_element_type=jnp.float32)
    send_pick = jnp.broadcast_to(
        send_pick[:, :, None, :], (owners, slot_count, steps_len, EMB_DEV)
    ).astype(jnp.bfloat16)
    rows_in = lax.all_to_all(send_rows, "emb", split_axis=0, concat_axis=0, tiled=True)
    pick_in = lax.all_to_all(send_pick, "emb", split_axis=0, concat_axis=0, tiled=True)
    slot_weights = jnp.einsum(
        "nzj,jah->nzah", pick_in[:, :, 0, :], enc_w, preferred_element_type=jnp.float32
    ).astype(jnp.bfloat16)
    encoded_slots = jnp.einsum(
        "nzsa,nzah->nzsh", rows_in, slot_weights, preferred_element_type=jnp.float32
    ).astype(jnp.bfloat16)
    returned = lax.all_to_all(encoded_slots, "emb", split_axis=0, concat_axis=0, tiled=True)
    encoded_own = jnp.einsum(
        "cos,osxh->cxh", target, returned, preferred_element_type=jnp.float32
    ).astype(jnp.bfloat16)
    hidden_own = (
        encoded_own.astype(jnp.float32) + step_embedding(t_index, hidden_width)[:, None, :]
    ).astype(jnp.bfloat16)
    hidden_group = lax.all_gather(hidden_own, "emb", axis=0, tiled=True)
    flat_hidden = hidden_group.reshape(rows_group, hidden_width)
    queries = jnp.dot(flat_hidden, query_weight, preferred_element_type=jnp.float32)
    queries = queries.astype(jnp.bfloat16).reshape(group, steps_len, heads_here, HD)
    key_heads = key_acc.astype(jnp.bfloat16).reshape(group, context_len, heads_here, HD)
    value_heads = value_acc.astype(jnp.bfloat16).reshape(group, context_len, heads_here, HD)
    scores = (
        jnp.einsum("gshd,gkhd->ghsk", queries, key_heads, preferred_element_type=jnp.float32)
        * scale
    )
    raised = jnp.exp(scores)
    probs = raised / jnp.sum(raised, axis=-1, keepdims=True)
    attended = jnp.einsum(
        "ghsk,gkhd->gshd",
        probs.astype(jnp.bfloat16),
        value_heads,
        preferred_element_type=jnp.float32,
    )
    attended = attended.astype(jnp.bfloat16).reshape(rows_group, columns)
    mixed = lax.dot_general(
        attended, out_weight, (((1,), (1,)), ((), ())), preferred_element_type=jnp.float32
    )
    own_rows = (jnp.arange(group) // per_device == position).astype(jnp.float32)
    branch = mixed.reshape(group, steps_len, hidden_width) + own_rows[
        :, None, None
    ] * hidden_group.astype(jnp.float32)
    dec_spans = dec_group[ids_group].astype(jnp.float32)
    partial_pred = jnp.einsum("csh,cha->csa", branch, dec_spans, precision=lax.Precision.HIGHEST)
    predicted = lax.psum(partial_pred, "emb")
    velocity = act_group.astype(jnp.float32) - noise_group.astype(jnp.float32)
    embodiments = act_dims.shape[0]
    dims_group = jnp.sum(
        jnp.where(ids_group[:, None] == jnp.arange(embodiments)[None, :], act_dims[None, :], 0),
        axis=1,
    )
    valid = (
        (jnp.arange(steps_len)[None, :, None] < length_group[:, None, None])
        & (jnp.arange(action_width)[None, None, :] < dims_group[:, None, None])
    ).astype(jnp.float32)
    error_rows = predicted - velocity
    length_float = length_group.astype(jnp.float32)
    loss_group = jnp.sum(valid * error_rows * error_rows, axis=(1, 2)) / length_float
    d_predicted = 2.0 * valid * error_rows / length_float[:, None, None]
    d_branch = jnp.einsum("csa,cha->csh", d_predicted, dec_spans, precision=lax.Precision.HIGHEST)
    d_branch = d_branch.astype(jnp.bfloat16).reshape(rows_group, hidden_width)
    d_out_part = lax.dot_general(
        attended, d_branch, (((0,), (0,)), ((), ())), preferred_element_type=jnp.float32
    )
    d_attended = jnp.dot(d_branch, out_weight, preferred_element_type=jnp.float32)
    d_attended = d_attended.astype(jnp.bfloat16).reshape(group, steps_len, heads_here, HD)
    d_probs = jnp.einsum(
        "gshd,gkhd->ghsk", d_attended, value_heads, preferred_element_type=jnp.float32
    )
    centre = jnp.sum(probs * d_probs, axis=-1, keepdims=True)
    d_scores = probs * (d_probs - centre)
    d_queries = jnp.einsum("ghsk,gkhd->gshd", d_scores, key_heads.astype(jnp.float32)) * scale
    d_queries = d_queries.astype(jnp.bfloat16).reshape(rows_group, columns)
    d_query_part = lax.dot_general(
        d_queries, flat_hidden, (((0,), (0,)), ((), ())), preferred_element_type=jnp.float32
    )
    d_query_total, d_out_total = lax.psum((d_query_part, d_out_part), "dp")
    loss_own = lax.dynamic_slice_in_dim(loss_group, position * per_device, per_device, 0)
    return (d_query_total, d_out_total, loss_own)


def solution(mesh):
    in_specs = (
        P(("dp", "emb"), None, None),
        P(("dp", "emb"), None, None),
        P(("dp", "emb")),
        P(("dp", "emb")),
        P(("dp", "emb")),
        P(),
        P("dp", None, "emb"),
        P("emb", None, None),
        P("emb", None, None),
        P("dp", "emb"),
        P("dp", "emb"),
        P("dp", "emb"),
        P("dp", "emb"),
    )
    out_specs = (P("emb", None), P("emb", None), P(("dp", "emb")))
    return jax.shard_map(body, mesh=mesh, in_specs=in_specs, out_specs=out_specs, check_vma=False)
```

profile of v0, /device:TPU:2, one launch (start us, length us, event | category | flops | bytes accessed | tf_op | source)
XLA Modules:
  0.0 569.5 jit_solution(8906377764032950270)
XLA Ops:
  7.2 0.7 all-gather.6.cloned.1.call-update
  8.0 0.7 all-gather.12.cloned.1.call-update
  8.7 0.7 all-gather.8.cloned.1.call-update
  9.4 0.7 and_select_fusion.3
  10.1 0.2 fusion.51
  10.3 0.3 convolution_convert_fusion.8
  10.6 0.7 broadcast_in_dim.12
  11.3 9.2 %all-to-all-start.1 = ((bf16[8,1,64,3]{2,3,1,0:T(4,128)(2,1)}), bf16[8,1,64,3]{2,3,1,0:T(4,128)(2,1)S(1)}, u32[]{:S(2)}, u32[]{:S(2)}) async-start(bf16[8,1,64,3]{2,3,1,0:T(4,128)(2,1)} %broadcast_in_dim.12), calls=%async_computation.1 | async-start | bytes 16384 | tf_op jit(solution)/shard_map/all_to_all | solution.py:82
  20.4 0.7 broadcast_subtract_fusion
  21.1 0.9 add_convert_fusion
  22.0 0.3 fusion.15
  22.3 0.8 reshape.236
  23.1 1.2 all-to-all-done.1
  24.3 4.7 all-to-all-start
  29.2 0.7 convolution_convert_fusion.2
  29.9 4.0 all-to-all-done
  34.0 2.5 fusion.2
  36.5 5.1 all-to-all-start.2
  41.8 19.9 %all-to-all-done.2 = bf16[8,1,64,1536]{3,2,1,0:T(8,128)(2,1)S(1)} async-done(((bf16[8,1,64,1536]{3,2,1,0:T(8,128)(2,1)}), bf16[8,1,64,1536]{3,2,1,0:T(8,128)(2,1)S(1)}, u32[]{:S(2)}, u32[]{:S(2)}) %all-to-all-start.2) | async-done | bytes 1572896 | tf_op jit(solution)/shard_map/all_to_all | solution.py:89
  61.8 1.2 fusion.5
  62.9 0.8 copy.72
  63.8 0.5 all-gather.14.cloned.1.call-update
  64.4 1.3 dynamic-slice
  66.3 0.2 dynamic-update-slice.1
  66.6 0.2 dynamic-update-slice
  66.8 7.3 %all-reduce.2 = (s32[16]{0:T(128)S(1)}, s32[16]{0:T(128)S(1)}) all-reduce(s32[16]{0:T(128)S(1)} %dynamic-update-slice.1, s32[16]{0:T(128)S(1)} %dynamic-update-slice), channel_id=1, replica_groups=mesh['dp'=64,'emb'=8] {'emb'}, use_global_device_ids=true, to_apply=%add.1 | all-reduce | flops 32 | bytes 256
  74.3 53.9 %all_gather.36 = bf16[1536,192]{1,0:T(8,128)(2,1)S(1)} all-gather(bf16[24,192]{1,0:T(8,128)(2,1)S(1)} %copy-done.11), channel_id=1, replica_groups=mesh['dp'=64,'emb'=8] {'dp'}, dimensions={0}, use_global_device_ids=true | all-gather | bytes 599040 | tf_op jit(solution)/shard_map/all_gather | solution.py:39
  128.2 48.9 %all_gather.40 = bf16[1536,192]{1,0:T(8,128)(2,1)S(1)} all-gather(bf16[24,192]{1,0:T(8,128)(2,1)S(1)} %copy-done.12), channel_id=1, replica_groups=mesh['dp'=64,'emb'=8] {'dp'}, dimensions={0}, use_global_device_ids=true | all-gather | bytes 599040 | tf_op jit(solution)/shard_map/all_gather | solution.py:42
  177.2 3.9 fusion.19
  181.1 0.9 copy.75
  182.0 0.8 reshape.209
  182.8 34.2 %all-gather.8.cloned.1.call-done = bf16[5120,192]{1,0:T(8,128)(2,1)} async-done(((bf16[80,192]{1,0:T(8,128)(2,1)}), bf16[5120,192]{1,0:T(8,128)(2,1)}) %all-gather.8.cloned.1.call-update) | async-done | bytes 1966096 | tf_op jit(solution)/shard_map/all_gather | solution.py:40
  217.0 2.8 fusion.16
  219.9 0.8 reshape.203
  220.6 27.7 %all-gather.10.cloned.1.call-done = bf16[16,64,1536]{2,1,0:T(8,128)(2,1)} async-done(((bf16[2,64,1536]{2,1,0:T(8,128)(2,1)}), bf16[16,64,1536]{2,1,0:T(8,128)(2,1)}) %all-gather.10.cloned.1.call-update) | async-done | bytes 3145744 | tf_op jit(solution)/shard_map/all_gather | solution.py:96
  248.3 3.1 convolution_convert_fusion.6
  251.4 0.5 reshape.208
  251.9 1.2 fusion.14
  253.2 0.4 convolution_convert_fusion.4
  253.6 0.8 copy.77
  254.5 6.7 %multiply_add_fusion = f32[16,64,1536]{2,0,1:T(8,128)} fusion(bf16[16,64,192]{2,0,1:T(8,128)(2,1)S(1)} %copy.77, bf16[16,64,1536]{2,1,0:T(8,128)(2,1)} %all-gather.10.cloned.1.call-done, f32[16]{0:T(128)S(1)} %compare_convert_fusion, bf16[1536,192]{1,0:T(8,128)(2,1)S(1)} %all_gather.40), kind=kOutput, calls=%fused_computation.3 | convolution fusion | flops 608698368 | bytes 10420288 | tf_op jit(solution)/shard_map/dot_general | solution.py:115
  261.2 29.0 %all-gather.14.cloned.1.call-done = bf16[24,1536,64]{1,2,0:T(8,128)(2,1)} async-done(((bf16[3,1536,64]{1,2,0:T(8,128)(2,1)}), bf16[24,1536,64]{1,2,0:T(8,128)(2,1)}) %all-gather.14.cloned.1.call-update) | async-done | bytes 4718608 | tf_op jit(solution)/shard_map/all_gather | solution.py:58
  290.1 4.7 gather_fusion
  294.9 11.0 %fusion = f32[16,64,64]{2,1,0:T(8,128)} fusion(bf16[16,1536,64]{1,2,0:T(8,128)(2,1)} %gather_fusion, f32[16,64,1536]{2,0,1:T(8,128)} %multiply_add_fusion), kind=kOutput, calls=%fused_computation.1 | convolution fusion | flops 1207959552 | bytes 9699328 | tf_op jit(solution)/shard_map/csh,cha->csa/dot_general | solution.py:123
  306.0 12.0 %all_gather.43 = bf16[16,64,64]{2,1,0:T(8,128)(2,1)S(1)} all-gather(bf16[2,64,64]{2,1,0:T(8,128)(2,1)S(1)} %copy-done.6), channel_id=1, replica_groups=mesh['dp'=64,'emb'=8] {'emb'}, dimensions={0}, use_global_device_ids=true | all-gather | bytes 147456 | tf_op jit(solution)/shard_map/all_gather | solution.py:60
  318.0 12.9 %all_gather.42 = bf16[16,64,64]{2,1,0:T(8,128)(2,1)S(1)} all-gather(bf16[2,64,64]{2,1,0:T(8,128)(2,1)S(1)} %copy-done.7), channel_id=1, replica_groups=mesh['dp'=64,'emb'=8] {'emb'}, dimensions={0}, use_global_device_ids=true | all-gather | bytes 147456 | tf_op jit(solution)/shard_map/all_gather | solution.py:59
  330.9 0.5 copy.84
  331.4 0.5 reshape.213
  331.9 44.4 %all-reduce.7.cloned.1.call-done = f32[16,64,64]{2,1,0:T(8,128)} async-done(((f32[16,64,64]{2,1,0:T(8,128)}), f32[16,64,64]{2,1,0:T(8,128)}) %all-reduce.7.cloned.1.call-update) | async-done | bytes 262160 | tf_op jit(solution)/shard_map/psum | solution.py:124
  376.3 4.7 convolution_convert_fusion
  381.1 1.6 copy-done.1
  382.7 1.2 convolution_convert_fusion.5
  383.9 0.5 reshape.211
  384.4 0.3 fusion.23
  384.9 1.5 fusion.13
  386.4 0.5 copy.83
  386.9 0.5 reshape.212
  387.5 3.8 fusion.59
  391.3 1.8 fusion.60
  393.1 0.4 fusion.30
  393.5 0.6 dynamic_slice.3
  394.1 165.1 %all-reduce.9.cloned.1.call-done = (f32[192,1536]{1,0:T(8,128)}, f32[192,1536]{1,0:T(8,128)}) async-done(((f32[192,1536]{1,0:T(8,128)}, f32[192,1536]{1,0:T(8,128)}), (f32[192,1536]{1,0:T(8,128)}, f32[192,1536]{1,0:T(8,128)})) %all-reduce.9.cloned.1.call-update) | async-done | bytes 2359312 | tf_op jit(solution)/shard_map/psum | solution.py:156
  559.2 2.5 copy.116
  561.7 1.0 copy.117
  (69 shorter events, 1.5 us)
Async XLA Ops:
  7.2 22.0 %copy-start = (bf16[3,64,1536]{2,1,0:T(8,128)(2,1)S(1)}, bf16[3,64,1536]{2,1,0:T(8,128)(2,1)}, u32[]{:S(2)}) copy-start(bf16[3,64,1536]{2,1,0:T(8,128)(2,1)} %param.20) | copy-start | bytes 1769476
  7.2 170.0 %all-gather.6.cloned.1.call-start = ((), (), s32[]{:S(2)}) async-start(), calls=%async_computation.3 | async-start | bytes 1474560 | tf_op jit(solution)/shard_map/all_gather | solution.py:52
  7.9 169.3 %all-gather.12.cloned.1.call-start = ((), (), s32[]{:S(2)}) async-start(), calls=%async_computation.6 | async-start | bytes 2662400 | tf_op jit(solution)/shard_map/all_gather | solution.py:41
  8.7 208.3 %all-gather.8.cloned.1.call-start = ((), (), s32[]{:S(2)}) async-start(), calls=%async_computation.4 | async-start | bytes 2662400 | tf_op jit(solution)/shard_map/all_gather | solution.py:40
  11.3 13.0 %all-to-all-start.1 = ((bf16[8,1,64,3]{2,3,1,0:T(4,128)(2,1)}), bf16[8,1,64,3]{2,3,1,0:T(4,128)(2,1)S(1)}, u32[]{:S(2)}, u32[]{:S(2)}) async-start(bf16[8,1,64,3]{2,3,1,0:T(4,128)(2,1)} %broadcast_in_dim.12), calls=%async_computation.1 | async-start | bytes 16384 | tf_op jit(solution)/shard_map/all_to_all | solution.py:82
  24.3 9.5 %all-to-all-start = ((bf16[8,2,2048]{2,1,0:T(2,128)(2,1)}), bf16[8,2,2048]{2,1,0:T(2,128)(2,1)S(1)}, u32[]{:S(2)}, u32[]{:S(2)}) async-start(bf16[8,2,2048]{2,1,0:T(2,128)(2,1)} %reshape.236), calls=%async_computation | async-start | bytes 131072 | tf_op jit(solution)/shard_map/all_to_all | solution.py:81
  34.0 7.6 %copy-start.13 = (s32[2]{0:T(128)S(1)}, s32[2]{0:T(128)}, u32[]{:S(2)}) copy-start(s32[2]{0:T(128)} %param.17) | copy-start | bytes 28
  36.5 29.9 %copy-start.14 = (s32[2]{0:T(128)S(1)}, s32[2]{0:T(128)}, u32[]{:S(2)}) copy-start(s32[2]{0:T(128)} %param.15) | copy-start | bytes 28
  36.5 30.1 %copy-start.15 = (s32[2]{0:T(128)S(1)}, s32[2]{0:T(128)}, u32[]{:S(2)}) copy-start(s32[2]{0:T(128)} %param.16) | copy-start | bytes 28
  36.5 37.7 %copy-start.16 = (s32[24]{0:T(128)S(1)}, s32[24]{0:T(128)}, u32[]{:S(2)}) copy-start(s32[24]{0:T(128)} %param.18) | copy-start | bytes 292
  36.5 37.9 %copy-start.11 = (bf16[24,192]{1,0:T(8,128)(2,1)S(1)}, bf16[24,192]{1,0:T(8,128)(2,1)}, u32[]{:S(2)}) copy-start(bf16[24,192]{1,0:T(8,128)(2,1)} %param.22) | copy-start | bytes 27652
  36.5 25.3 %all-to-all-start.2 = ((bf16[8,1,64,1536]{3,2,1,0:T(8,128)(2,1)}), bf16[8,1,64,1536]{3,2,1,0:T(8,128)(2,1)S(1)}, u32[]{:S(2)}, u32[]{:S(2)}) async-start(bf16[8,1,64,1536]{3,2,1,0:T(8,128)(2,1)} %fusion.2), calls=%async_computation.2 | async-start | bytes 3145728 | tf_op jit(solution)/shard_map/all_to_all | solution.py:89
  41.6 86.6 %copy-start.12 = (bf16[24,192]{1,0:T(8,128)(2,1)S(1)}, bf16[24,192]{1,0:T(8,128)(2,1)}, u32[]{:S(2)}) copy-start(bf16[24,192]{1,0:T(8,128)(2,1)} %param.25) | copy-start | bytes 27652
  41.6 206.7 %all-gather.10.cloned.1.call-start = ((), (), s32[]{:S(2)}) async-start(), calls=%async_computation.5 | async-start | bytes 3538944 | tf_op jit(solution)/shard_map/all_gather | solution.py:96
  63.8 226.4 %all-gather.14.cloned.1.call-start = ((), (), s32[]{:S(2)}) async-start(), calls=%async_computation.7 | async-start | bytes 5308416 | tf_op jit(solution)/shard_map/all_gather | solution.py:58
  64.3 312.0 %all-reduce.7.cloned.1.call-start = ((), (), s32[]{:S(2)}) async-start(), calls=%async_computation.8 | async-start | bytes 1048576 | tf_op jit(solution)/shard_map/psum | solution.py:124
  177.2 39.8 %copy-start.3 = (bf16[16,8,5120]{2,1,0:T(8,128)(2,1)S(1)}, bf16[16,8,5120]{2,1,0:T(8,128)(2,1)}, u32[]{:S(2)}) copy-start(bf16[16,8,5120]{2,1,0:T(8,128)(2,1)} %all-gather.6.cloned.1.call-done) | copy-start | bytes 3932164
  248.3 4.9 copy-start.8
  253.2 8.0 %copy-start.17 = (f32[16,4,64,8]{2,3,1,0:T(8,128)}, f32[16,4,64,8]{2,3,1,0:T(8,128)S(1)}, u32[]{:S(2)}) copy-start(f32[16,4,64,8]{2,3,1,0:T(8,128)S(1)} %fusion.14) | copy-start | bytes 393220
  294.8 11.2 %copy-start.6 = (bf16[2,64,64]{2,1,0:T(8,128)(2,1)S(1)}, bf16[2,64,64]{2,1,0:T(8,128)(2,1)}, u32[]{:S(2)}) copy-start(bf16[2,64,64]{2,1,0:T(8,128)(2,1)} %param.14) | copy-start | bytes 49156
  294.8 23.2 %copy-start.7 = (bf16[2,64,64]{2,1,0:T(8,128)(2,1)S(1)}, bf16[2,64,64]{2,1,0:T(8,128)(2,1)}, u32[]{:S(2)}) copy-start(bf16[2,64,64]{2,1,0:T(8,128)(2,1)} %param.13) | copy-start | bytes 49156
  305.9 253.3 %all-reduce.9.cloned.1.call-start = ((), (), s32[]{:S(2)}) async-start(), calls=%async_computation.9 | async-start | bytes 4718592 | tf_op jit(solution)/shard_map/psum | solution.py:156
  381.1 1.6 copy-start.1
  381.1 3.3 copy-start.9
  382.7 2.0 copy-start.18
  382.7 2.2 copy-start.10
  387.4 3.8 copy-start.2
  391.3 1.8 copy-start.4
  559.2 2.5 copy-start.5
Sparse Core Ops, SparseCore 0:
  10.1 32.8 all-gather.5
  46.1 86.9 all-gather.11
  136.1 80.8 all-gather.7
  219.5 28.7 all-gather.9
  250.3 39.7 all-gather.13
  306.0 70.2 all-reduce.6
  393.2 165.9 all-reduce.8
where the time goes:
time: 570 us
  waiting for transfers between devices  328 us (58%)
  blocking collectives  135 us (24%)
  matrix products  47.3 us (8%)
  local copies, waits for them, and re-layouts  21.3 us (4%)
  starting transfers between devices  19.2 us (3%)
  between operations  15.1 us (3%)
    psum x1, waiting for transfers between devices, body(): d_query_total, d_out_total = lax.psum((d_query_part, d_out_part), 'dp')  165 us
    all_gather x1, blocking collectives, body(): lax.all_gather(wq, 'dp', axis=0, tiled=True)  53.9 us
    all_gather x1, blocking collectives, body(): lax.all_gather(wo_t, 'dp', axis=0, tiled=True)  48.9 us
    psum x1, waiting for transfers between devices, body(): predicted = lax.psum(partial_pred, 'emb')  44.4 us
    all_gather x1, waiting for transfers between devices, body(): lax.all_gather(wk, 'dp', axis=0, tiled=True)  34.2 us
    all_gather x1, waiting for transfers between devices, body(): lax.all_gather(dec_w, 'emb', axis=0, tiled=True)  29 us
    all_gather x1, waiting for transfers between devices, body(): hidden_group = lax.all_gather(hidden_own, 'emb', axis=0, tiled=True)  27.7 us
    all_to_all x1, waiting for transfers between devices, body(): lax.all_to_all(encoded_slots, 'emb', split_axis=0, concat_axis=0, tiled=T...  19.9 us
  transfers between devices with their start and end apart: 10, of which 8 were waited for; matrix products, arithmetic and copies ran while one was open for 6% of the time, Pallas kernels for 0%

commit v1 on v0

v1 whole, which is shorter than its diff:
```python
import functools
import math

import jax
import jax.numpy as jnp
from jax import lax
from jax.experimental import pallas as pl
from jax.experimental.pallas import tpu as pltpu
from jax.sharding import PartitionSpec as P

HD = 48
TSTEPS = 1000
H = 1536
HC = 192
STEPS = 64
EMBS = 24
NY = 8
NZ = 8
NX = 4
GROUP = 16
CTX = 8
ROWS = GROUP * STEPS
KA = 64
KB = 48
MESH = pl.DeviceIdType.MESH
BF = jnp.bfloat16
F32 = jnp.float32
NT = (((1,), (1,)), ((), ()))


def mm(a, b):
    return jnp.dot(a, b, preferred_element_type=F32)


def mm_nt(a, b):
    return lax.dot_general(a, b, NT, preferred_element_type=F32)


class Copies:
    def __init__(self, send, recv):
        self.send, self.recv, self.count, self.made = send, recv, 0, []

    def make(self, src, dst, device):
        k = self.count
        self.count += 1
        copy = pltpu.make_async_remote_copy(
            src_ref=src, dst_ref=dst, send_sem=self.send.at[k], recv_sem=self.recv.at[k],
            device_id=device, device_id_type=MESH,
        )
        copy.start()
        self.made.append(copy)
        return copy


N_COPIES = 256


def kernel(
    wa_in, wb_in, f_in, enc_in, dec_in, nz_in, vel_in, meta_in, code_in, ids_in,
    gq_out, go_out, loss_out,
    wa, wb, fg, eg, dg, nzg, cg, ig, ids, kv, qo, wq, wo, kb, vb,
    hid, dbr, prs, att, att_t, dq_t, ps, pr, dp_own, dpg,
    gs, gr, sb, sr, fs, sg, og, send_sems, recv_sems, local_sem,
):
    i = lax.axis_index("dp")
    j = lax.axis_index("emb")
    y, z = i // NZ, i % NZ
    x, c = j // 2, j % 2
    ne = 2 * NX

    barrier = pltpu.get_barrier_semaphore()
    for k in range(1, ne):
        pl.semaphore_signal(barrier, inc=1, device_id=(i, (j + k) % ne), device_id_type=MESH)
    for k in range(1, NY):
        pl.semaphore_signal(barrier, inc=1, device_id=(((y + k) % NY) * NZ + z, j), device_id_type=MESH)
    for k in range(1, NZ):
        pl.semaphore_signal(barrier, inc=1, device_id=(y * NZ + (z + k) % NZ, j), device_id_type=MESH)
    pl.semaphore_wait(barrier, (ne - 1) + (NY - 1) + (NZ - 1))

    cs = Copies(send_sems, recv_sems)
    go = cs.make
    dev_y = lambda t: (t * NZ + z, j)
    dev_z = lambda t: (y * NZ + t, j)
    dev_e = lambda t: (i, t)
    fwd = 1 - 2 * c

    small = []
    for k in range(1, ne):
        peer = dev_e((j + k) % ne)
        small.append(go(nz_in, nzg.at[j], peer))
        small.append(go(code_in, cg.at[j], peer))
        small.append(go(ids_in, ig.at[j], peer))

    def ring(step, me, device, first, block, heavy, light):
        up = device((me + fwd + 8) % 8)
        down = device((me - fwd + 8) % 8)
        out = []
        if step <= heavy:
            b = (me - fwd * (step - 1) + 16) % 8
            for src, dst in zip(first if step == 1 and first else block(b), block(b)):
                out.append(go(src, dst, up))
        if step <= light:
            b = (me + fwd * (step - 1) + 16) % 8
            for src, dst in zip(first if step == 1 and first else block(b), block(b)):
                out.append(go(src, dst, down))
        return out

    def arrive(copies):
        for copy in copies:
            copy.wait_recv()

    a1 = lambda s: ring(s, z, dev_z, [wa_in], lambda b: [wa.at[y, b]], 4, 3)
    b1 = lambda s: ring(s, y, dev_y, [wb_in], lambda b: [wb.at[z, b]], 4, 3)
    a2 = lambda s: ring(s, y, dev_y, None, lambda b: [wa.at[b, pl.ds(0, 4)], wa.at[b, pl.ds(4, 4)]], 4, 3)
    b2 = lambda s: ring(s, z, dev_z, None, lambda b: [wb.at[b, pl.ds(0, 4)], wb.at[b, pl.ds(4, 4)]], 4, 3)

    right, left = (2 * ((x + 1) % NX) + c), (2 * ((x + 3) % NX) + c)
    opposite, sibling = (2 * ((x + 2) % NX) + c), (2 * x + 1 - c)

    def along_x_start(whole_in, half_in, half, whole):
        r0 = go(half_in(0), half(j, 0), dev_e(right))
        l1 = go(half_in(1), half(j, 1), dev_e(left))
        r1 = go(half_in(1), half(j, 1), dev_e(right))
        l0 = go(half_in(0), half(j, 0), dev_e(left))
        s = go(whole_in, whole(j), dev_e(sibling))
        return r0, l1, r1, l0, s

    def along_x_forward(first, half, whole):
        r0, l1, r1, l0, s = first
        r0.wait_recv()
        f0 = go(half(left, 0), half(left, 0), dev_e(right))
        l1.wait_recv()
        f1 = go(half(right, 1), half(right, 1), dev_e(left))
        r1.wait_recv()
        s0 = go(whole(left), whole(left), dev_e(sibling))
        l0.wait_recv()
        s1 = go(whole(right), whole(right), dev_e(sibling))
        return f0, f1, s0, s1, s

    def along_x_last(second, half, whole):
        f0, f1, s0, s1, s = second
        f0.wait_recv()
        f1.wait_recv()
        s2 = go(whole(opposite), whole(opposite), dev_e(sibling))
        return s, s0, s1, s2

    f_half = lambda b, h: fg.at[b, pl.ds(64 * h, 64)]
    f_whole = lambda b: fg.at[b]
    w3 = lambda buf: (
        (lambda b, h: buf.at[pl.ds(3 * b, 3), pl.ds(32 * h, 32)]),
        (lambda b: buf.at[pl.ds(3 * b, 3)]),
    )
    e_half, e_whole = w3(eg)
    d_half, d_whole = w3(dg)

    ra, rb = a1(1), b1(1)
    fx = along_x_start(f_in, lambda h: f_in.at[pl.ds(64 * h, 64)], f_half, f_whole)
    ex = along_x_start(enc_in, lambda h: enc_in.at[:, pl.ds(32 * h, 32)], e_half, e_whole)

    wa[y, z] = wa_in[...]
    wb[z, y] = wb_in[...]
    fg[j] = f_in[...]
    eg[pl.ds(3 * j, 3)] = enc_in[...]
    dg[pl.ds(3 * j, 3)] = dec_in[...]
    nzg[j] = nz_in[...]
    cg[j] = code_in[...]
    ig[j] = ids_in[...]

    for step in (2, 3, 4):
        arrive(ra)
        ra = a1(step)
        arrive(rb)
        rb = b1(step)
    fx = along_x_forward(fx, f_half, f_whole)
    arrive(ra)
    ra = a2(1)
    arrive(rb)
    rb = b2(1)
    fx = along_x_last(fx, f_half, f_whole)
    arrive(small)
    table = pltpu.make_async_copy(ig, ids, local_sem)
    table.start()
    table.wait()
    arrive(fx)

    def kv_part(b):
        return mm(fg[b][:, : 8 * KA], wa[b].reshape(8 * KA, 2 * HC))

    kv[...] = kv_part(y)
    for step in (2, 3, 4):
        arrive(ra)
        ra = a2(step)
        arrive(rb)
        rb = b2(step)
        kv[...] += kv_part((y - fwd * (step - 1) + 16) % 8)
        kv[...] += kv_part((y + fwd * (step - 1) + 16) % 8)
        if step == 2:
            ex = along_x_forward(ex, e_half, e_whole)
            dx = along_x_start(dec_in, lambda h: dec_in.at[:, pl.ds(32 * h, 32)], d_half, d_whole)
        if step == 3:
            ex = along_x_last(ex, e_half, e_whole)
    arrive(ra)
    arrive(rb)
    kv[...] += kv_part((y + 4) % 8)
    for b in range(8):
        kv[...] += mm(fg[b][:, 8 * KA :], wb[:, b, 0:16, :].reshape(128, 2 * HC))

    def unpack(zz, carry):
        for yy in range(NY):
            qo[yy * NZ + zz] = wb[zz, yy, 16:40, :].astype(F32)
        return carry

    lax.fori_loop(0, NZ, unpack, 0)

    def split(b, carry):
        rows = qo[pl.ds(8 * b, 8)].reshape(HC, 2 * HC)
        wq[pl.ds(pl.multiple_of(HC * b, HC), HC), :] = rows[:, :HC].astype(BF)
        wo[pl.ds(pl.multiple_of(HC * b, HC), HC), :] = rows[:, HC:].astype(BF)
        return carry

    lax.fori_loop(0, NY, split, 0)

    head_of_row = lax.broadcasted_iota(jnp.int32, (32, HC), 0) >> 3
    column = lax.broadcasted_iota(jnp.int32, (32, HC), 1)
    low = head_of_row * HD
    head_mask = jnp.where((column >= low) & (column < low + HD), 1.0, 0.0).astype(F32)

    def spread(flat):
        three = flat.astype(BF).astype(F32).reshape(GROUP, CTX, HC)
        return (jnp.concatenate([three] * 4, axis=1) * head_mask[None]).astype(BF)

    kb[...] = spread(kv[:, :HC])
    vb[...] = spread(kv[:, HC:])

    same_head = jnp.where(
        (lax.broadcasted_iota(jnp.int32, (32, 32), 0) >> 3)
        == (lax.broadcasted_iota(jnp.int32, (32, 32), 1) >> 3), 1.0, 0.0,
    ).astype(F32)

    def head_sum(values):
        return jnp.dot(values, same_head, precision=lax.Precision.HIGHEST, preferred_element_type=F32)

    arrive(ex)
    dx = along_x_forward(dx, d_half, d_whole)
    lane = lax.broadcasted_iota(jnp.int32, (STEPS, 2 * STEPS), 1)
    scale = 1.0 / math.sqrt(HD)

    def two_spans(pair):
        zero = jnp.zeros_like(pair)
        return jnp.concatenate([jnp.where(lane < STEPS, pair, zero), jnp.where(lane >= STEPS, pair, zero)], axis=0)

    def weights_of(buf, p):
        return jnp.concatenate([buf[ids[p, 0, 0]], buf[ids[p, 0, 1]]], axis=0)

    def encode(p, carry):
        enc = mm(two_spans(nzg[p]), weights_of(eg, p)).astype(BF).astype(F32)
        code = cg[p]
        for q in range(2):
            row = jnp.concatenate([code[4 * q + r : 4 * q + r + 1] for r in range(4)], axis=1)
            hid[pl.ds(pl.multiple_of(p * 128 + 64 * q, 64), 64), :] = (enc[64 * q : 64 * q + 64] + row).astype(BF)
        return carry

    lax.fori_loop(0, ne, encode, 0)

    def attend(g, carry):
        here = pl.ds(pl.multiple_of(256 * g, 256), 256)
        queries = mm(hid[here, :], wq[...]).astype(BF)
        scores = jnp.concatenate([mm_nt(queries[64 * s : 64 * s + 64], kb[4 * g + s]) for s in range(4)], axis=0) * scale
        raised = jnp.exp(scores)
        probs = raised / head_sum(raised)
        prs[here, :] = probs
        rounded = probs.astype(BF)
        out = jnp.concatenate([mm(rounded[64 * s : 64 * s + 64], vb[4 * g + s]) for s in range(4)], axis=0)
        att[here, :] = out.astype(BF)
        att_t[:, here] = out.T.astype(BF)
        return carry

    lax.fori_loop(0, 4, attend, 0)
    dx = along_x_last(dx, d_half, d_whole)
    arrive(dx)

    def decode(p, carry):
        here = pl.ds(pl.multiple_of(128 * p, 128), 128)
        own = jnp.where(p == j, 1.0, 0.0).astype(F32)
        branch = (mm_nt(att[here, :], wo[...]) + own * hid[here, :].astype(F32)).astype(BF)
        ps[p] = jnp.concatenate(
            [mm_nt(branch[64 * q : 64 * q + 64], dg[ids[p, 0, q]]) for q in range(2)], axis=1
        ).astype(BF)
        return carry

    lax.fori_loop(0, ne, decode, 0)

    shares = [go(ps.at[(j + k) % ne], pr.at[k - 1], dev_e((j + k) % ne)) for k in range(1, ne)]
    arrive(shares)
    predicted = ps[j].astype(F32)
    for k in range(1, ne):
        predicted += pr[k - 1].astype(F32)
    length, dims = meta_in[0:1, :], meta_in[1:2, :]
    step_row = lax.broadcasted_iota(jnp.int32, (STEPS, 2 * STEPS), 0).astype(F32)
    step_col = (lane & (STEPS - 1)).astype(F32)
    valid = jnp.where((step_row < length) & (step_col < dims), 1.0, 0.0).astype(F32)
    error = predicted - vel_in[...]
    squares = jnp.sum(valid * error * error, axis=0, keepdims=True)
    low_lane = lane[0:1] < STEPS
    for q in range(2):
        one = jnp.sum(jnp.where(low_lane == (q == 0), squares, 0.0), axis=1, keepdims=True)
        loss_out[q : q + 1, :] = one / length[:, 64 * q : 64 * q + 1] + jnp.zeros((1, 128), F32)
    dp_own[...] = (2.0 * valid * error / length).astype(BF)
    errors = [go(dp_own, dpg.at[j], dev_e((j + k) % ne)) for k in range(1, ne)]
    dpg[j] = dp_own[...]
    arrive(errors)

    def d_branch(p, carry):
        here = pl.ds(pl.multiple_of(128 * p, 128), 128)
        dbr[here, :] = mm(two_spans(dpg[p]), weights_of(dg, p)).astype(BF)
        return carry

    lax.fori_loop(0, ne, d_branch, 0)

    def slice_of(left_t, right_rows, t):
        rows = pl.ds(pl.multiple_of(96 * (t // 4), 16), 96)
        columns = pl.ds(pl.multiple_of(384 * (t % 4), 128), 384)
        return mm(left_t[rows, :], right_rows[:, columns])

    def scatter(n, left_t, right_rows, me, device):
        out = []
        for k in range(1, 8):
            t = (me + k) % 8
            gs[n, k - 1] = slice_of(left_t, right_rows, t).astype(BF)
            out.append(go(gs.at[n, k - 1], gr.at[n, k - 1], device(t)))
        return out

    go_copies = scatter(1, att_t, dbr, z, dev_z)

    def back(g, carry):
        here = pl.ds(pl.multiple_of(256 * g, 256), 256)
        d_att = mm(dbr[here, :], wo[...]).astype(BF)
        d_probs = jnp.concatenate([mm_nt(d_att[64 * s : 64 * s + 64], vb[4 * g + s]) for s in range(4)], axis=0)
        probs = prs[here, :]
        d_scores = (probs * (d_probs - head_sum(probs * d_probs))).astype(BF)
        out = jnp.concatenate([mm(d_scores[64 * s : 64 * s + 64], kb[4 * g + s]) for s in range(4)], axis=0) * scale
        dq_t[:, here] = out.T.astype(BF)
        return carry

    lax.fori_loop(0, 4, back, 0)
    gq_copies = scatter(0, dq_t, hid, y, dev_y)

    def add_up(n, copies, left_t, right_rows, me, me2, device2):
        total = slice_of(left_t, right_rows, me)
        arrive(copies)
        for k in range(7):
            total += gr[n, k].astype(F32)
        sb[n, 0:96] = total.astype(BF)
        sb[n, 96:128] = jnp.zeros((32, 384), BF)
        out = []
        for k in range(1, 8):
            t = (me2 + k) % 8
            out.append(go(sb.at[n, pl.ds(pl.multiple_of(16 * t, 16), 16)], sr.at[n, k - 1], device2(t)))
        return out

    def finish(n, copies, me2, device2):
        arrive(copies)
        total = sb[n, pl.ds(pl.multiple_of(16 * me2, 16), 16)].astype(F32)
        for k in range(7):
            total += sr[n, k].astype(F32)
        fs[n] = total.astype(BF)
        out = [go(fs.at[n], sg.at[n, me2], device2((me2 + k) % 8)) for k in range(1, 8)]
        sg[n, me2] = fs[n]
        return out

    def gather(n, copies, me, device):
        arrive(copies)
        out = [go(sg.at[n, pl.ds(0, 6)], og.at[n, me], device((me + k) % 8)) for k in range(1, 8)]
        og[n, me] = sg[n, 0:6]
        return out

    go_copies = add_up(1, go_copies, att_t, dbr, z, y, dev_y)
    gq_copies = add_up(0, gq_copies, dq_t, hid, y, z, dev_z)
    go_copies = finish(1, go_copies, y, dev_y)
    gq_copies = finish(0, gq_copies, z, dev_z)
    go_copies = gather(1, go_copies, z, dev_z)
    gq_copies = gather(0, gq_copies, y, dev_y)
    arrive(go_copies)
    go_out[...] = og[1].reshape(8, 96, 384)
    arrive(gq_copies)
    gq_out[...] = og[0].reshape(8, 96, 384)
    for copy in cs.made:
        copy.wait_send()


def step_embedding(step_values, width):
    half = width // 2
    freq = jnp.exp(-math.log(10000.0) * jnp.arange(half, dtype=F32) / half)
    angle = step_values.astype(F32)[:, None] * freq[None, :]
    return jnp.concatenate([jnp.sin(angle), jnp.cos(angle)], axis=1)


def side_by_side(spans):
    return jnp.concatenate([spans[0], spans[1]], axis=1)


def body(actions, noise, emb_ids, lengths, t_index, act_dims, features, enc_w, dec_w, wq, wk, wv, wo_t):
    shard = jnp.concatenate(
        [jnp.concatenate([wk, wv], axis=1), jnp.concatenate([wq, wo_t], axis=1), jnp.zeros((8, 2 * HC), BF)], axis=0
    )
    flat = features.reshape(GROUP * CTX, 8, 80)
    feats = jnp.concatenate(
        [flat[:, :, :KA].reshape(GROUP * CTX, 8 * KA), flat[:, :, KA:].reshape(GROUP * CTX, 128)], axis=1
    )
    act, noi = actions.astype(F32), noise.astype(F32)
    fraction = (t_index.astype(F32) / TSTEPS)[:, None, None]
    noisy = side_by_side(((1.0 - fraction) * noi + fraction * act).astype(BF))
    velocity = side_by_side(act - noi)
    code = step_embedding(t_index, H).reshape(8, 384)
    dims = act_dims[emb_ids]
    meta = jnp.stack(
        [jnp.repeat(lengths, STEPS).astype(F32), jnp.repeat(dims, STEPS).astype(F32)] + [jnp.ones((128,), F32)] * 6
    )
    ids = jnp.zeros((8, 128), jnp.int32).at[0, 0:2].set(emb_ids)
    vm = pl.BlockSpec(memory_space=pltpu.VMEM)
    V = pltpu.VMEM
    d_q, d_o, loss = pl.pallas_call(
        kernel,
        out_shape=(
            jax.ShapeDtypeStruct((8, 96, 384), BF),
            jax.ShapeDtypeStruct((8, 96, 384), BF),
            jax.ShapeDtypeStruct((8, 128), F32),
        ),
        in_specs=[vm] * 10,
        out_specs=(vm, vm, vm),
        scratch_shapes=[
            V((NY, NZ, KA, 2 * HC), BF),
            V((NZ, NY, KB, 2 * HC), BF),
            V((8, GROUP * CTX, 640), BF),
            V((EMBS, STEPS, H), BF),
            V((EMBS, STEPS, H), BF),
            V((8, STEPS, 128), BF),
            V((8, 8, 384), F32),
            V((8, 8, 128), jnp.int32),
            pltpu.SMEM((8, 8, 128), jnp.int32),
            V((GROUP * CTX, 2 * HC), F32),
            V((64, 24, 2 * HC), F32),
            V((H, HC), BF),
            V((H, HC), BF),
            V((GROUP, 32, HC), BF),
            V((GROUP, 32, HC), BF),
            V((ROWS, H), BF),
            V((ROWS, H), BF),
            V((ROWS, 32), F32),
            V((ROWS, HC), BF),
            V((HC, ROWS), BF),
            V((HC, ROWS), BF),
            V((8, STEPS, 128), BF),
            V((7, STEPS, 128), BF),
            V((STEPS, 128), BF),
            V((8, STEPS, 128), BF),
            V((2, 7, 96, 384), BF),
            V((2, 7, 96, 384), BF),
            V((2, 128, 384), BF),
            V((2, 7, 16, 384), BF),
            V((2, 16, 384), BF),
            V((2, 8, 16, 384), BF),
            V((2, 8, 6, 16, 384), BF),
            pltpu.SemaphoreType.DMA((N_COPIES,)),
            pltpu.SemaphoreType.DMA((N_COPIES,)),
            pltpu.SemaphoreType.DMA,
        ],
        compiler_params=pltpu.CompilerParams(
            collective_id=0, has_side_effects=True, vmem_limit_bytes=56 * 1024 * 1024
        ),
    )(shard[:KA], shard[KA:], feats, enc_w, jnp.swapaxes(dec_w, 1, 2), noisy, velocity, meta, code, ids)

    def whole(slices):
        return slices.astype(F32).reshape(2, 4, 96, 384).transpose(0, 2, 1, 3).reshape(HC, H)

    return whole(d_q), whole(d_o), loss[0:2, 0]


def solution(mesh):
    rows = P(("dp", "emb"))
    in_specs = (
        P(("dp", "emb"), None, None), P(("dp", "emb"), None, None), rows, rows, rows, P(),
        P("dp", None, "emb"), P("emb", None, None), P("emb", None, None),
        P("dp", "emb"), P("dp", "emb"), P("dp", "emb"), P("dp", "emb"),
    )
    out_specs = (P("emb", None), P("emb", None), rows)
    return jax.shard_map(body, mesh=mesh, in_specs=in_specs, out_specs=out_specs, check_vma=False)
```

time: 570 us -> 168 us (0.29)
  the two profiles are of different devices: /device:TPU:2 before, /device:TPU:16 now
where the time goes in v1:
time: 168 us
  Pallas kernels  147 us (88%)
  other arithmetic  10.6 us (6%)
  local copies, waits for them, and re-layouts  9.22 us (5%)
    pallas_call x1, Pallas kernels, body(): pl.pallas_call(kernel, out_shape=(jax.ShapeDtypeStruct((8, 96, 384), BF),...  147 us

profile of v1, /device:TPU:16, one launch (start us, length us, event | category | flops | bytes accessed | tf_op | source)
XLA Modules:
  0.0 167.5 jit_solution(12491877211535086062)
XLA Ops:
  0.6 0.0 copy-start
  0.6 0.0 copy-start.2
  0.7 0.7 convert_element_type.47
  1.4 0.1 broadcast_in_dim.17
  1.4 0.1 convert_element_type.48
  1.5 0.7 compare_select_fusion
  2.2 0.7 convert_element_type.43
  2.8 0.1 pad_slice_fusion
  2.9 0.1 pad.10.clone
  3.0 0.1 pad.9.clone
  3.1 0.7 broadcast_subtract_fusion
  3.7 0.0 copy-done
  3.7 0.6 gather_fusion
  4.4 0.1 broadcast_in_dim.19
  4.5 0.1 convert_element_type.50
  4.5 0.7 maximum_maximum_fusion.meta_in
  5.2 1.2 scatter.4.ids_in
  6.5 0.2 multiply_sine_fusion
  6.7 0.6 reshape.104.code_in
  7.3 1.4 fusion.3.wb_in
  8.7 1.5 pad_maximum_fusion.1.wa_in
  10.2 0.9 convert_subtract_fusion
  11.0 0.7 pad_maximum_fusion.4.vel_in
  11.7 0.7 pad_maximum_fusion.5.nz_in
  12.4 0.0 copy-done.2
  12.4 0.3 reshape.101
  12.7 0.2 copy.18
  12.9 0.1 copy.20
  13.0 0.1 slice.56
  13.2 0.2 copy.19
  13.3 0.1 copy.21
  13.5 0.7 pad_maximum_fusion.f_in
  14.2 146.9 %shard_map.148 = (bf16[8,96,384]{2,1,0:T(8,128)(2,1)}, bf16[8,96,384]{2,1,0:T(8,128)(2,1)}, f32[8,128]{1,0:T(8,128)}) custom-call(bf16[64,384]{1,0:T(8,128)(2,1)} %pad_maximum_fusion.1.wa_in, bf16[48,384]{1,0:T(8,128)(2,1)} %fusion.3.wb_in, bf16[128,640]{1,0:T(8,128)(2,1)} %pad_maximum_fusion.f_in, bf16[3,64,1536]{2,1,0:T(8,128)(2,1)} %enc_in.1, ...), custom_call_target="tpu_custom_call" | custom-call | tf_op jit(solution)/shard_map/pallas_call | solution.py:422
  161.1 1.3 slice_reduce_fusion
  162.4 1.1 convert_bitcast_fusion
  163.6 0.8 copy.23
  164.3 0.0 copy-start.1
  164.3 1.1 copy.25
  165.4 0.1 copy-done.1
  165.6 0.1 convert_bitcast_fusion.1
  165.6 0.8 copy.22
  166.4 1.1 copy.24
  (9 shorter events, 0.0 us)
Async XLA Ops:
  0.6 3.1 %copy-start = (s32[24]{0:T(128)S(1)}, s32[24]{0:T(128)}, u32[]{:S(2)}) copy-start(s32[24]{0:T(128)} %param.20) | copy-start | bytes 292
  0.6 11.8 %copy-start.2 = (bf16[16,8,640]{2,1,0:T(8,128)(2,1)S(1)}, bf16[16,8,640]{2,1,0:T(8,128)(2,1)}, u32[]{:S(2)}) copy-start(bf16[16,8,640]{2,1,0:T(8,128)(2,1)} %param.21) | copy-start | bytes 491524
  164.3 1.2 copy-start.1

commit v2 on v1

--- a/solution.py
+++ b/solution.py
@@ -20,8 +20,8 @@
 GROUP = 16
 CTX = 8
 ROWS = GROUP * STEPS
-KA = 64
-KB = 48
+RK = 80
+RB = 160
 MESH = pl.DeviceIdType.MESH
 BF = jnp.bfloat16
 F32 = jnp.float32
@@ -56,8 +56,9 @@
 
 
 def kernel(
-    wa_in, wb_in, f_in, enc_in, dec_in, nz_in, vel_in, meta_in, code_in, ids_in,
+    act, noise, emb_ids, lengths, levels, act_dims, f_in, enc_in, dec_in, wq_own, wk_own, wv_own, wo_own,
     gq_out, go_out, loss_out,
+    wa_in, wb_in, nz_in, vel_in, code_in, ids_in,
     wa, wb, fg, eg, dg, nzg, cg, ig, ids, kv, qo, wq, wo, kb, vb,
     hid, dbr, prs, att, att_t, dq_t, ps, pr, dp_own, dpg,
     gs, gr, sb, sr, fs, sg, og, send_sems, recv_sems, local_sem,
@@ -75,6 +76,31 @@
         pl.semaphore_signal(barrier, inc=1, device_id=(((y + k) % NY) * NZ + z, j), device_id_type=MESH)
     for k in range(1, NZ):
         pl.semaphore_signal(barrier, inc=1, device_id=(y * NZ + (z + k) % NZ, j), device_id_type=MESH)
+
+    wa_in[...] = jnp.concatenate([wk_own[...], wv_own[:, :STEPS]], axis=1)
+    wb_in[0:RK, :] = wv_own[:, STEPS:]
+    q_own, o_own = wq_own[...].astype(F32), wo_own[...].astype(F32)
+    wb_in[RK:RB, :] = jnp.concatenate(
+        [q_own[:, :128], jnp.concatenate([q_own[:, 128:], o_own[:, 128:]], axis=1), o_own[:, :128],
+         jnp.zeros((8, 128), F32)], axis=0,
+    ).astype(BF)
+    lane = lax.broadcasted_iota(jnp.int32, (STEPS, 2 * STEPS), 1)
+    mixed = []
+    for q in range(2):
+        fraction = jnp.full((STEPS, STEPS), levels[q].astype(F32), F32) / TSTEPS
+        mixed.append((1.0 - fraction) * noise[q].astype(F32) + fraction * act[q].astype(F32))
+    nz_in[...] = jnp.concatenate(mixed, axis=1).astype(BF)
+    vel_in[...] = jnp.concatenate([act[q].astype(F32) - noise[q].astype(F32) for q in range(2)], axis=1)
+    code_row = lax.broadcasted_iota(jnp.int32, (8, 384), 0)
+    code_lane = lax.broadcasted_iota(jnp.int32, (8, 384), 1)
+    half = H // 2
+    freq = jnp.exp(-math.log(10000.0) * (code_lane + 384 * (code_row & 1)).astype(F32) / half)
+    level = jnp.where(code_row < 4, levels[0].astype(F32), levels[1].astype(F32))
+    angle = level * freq
+    code_in[...] = jnp.where((code_row & 2) == 0, jnp.sin(angle), jnp.cos(angle))
+    id_lane = lax.broadcasted_iota(jnp.int32, (8, 128), 1)
+    ids_in[...] = jnp.where(id_lane == 0, emb_ids[0], emb_ids[1])
+
     pl.semaphore_wait(barrier, (ne - 1) + (NY - 1) + (NZ - 1))
 
     cs = Copies(send_sems, recv_sems)
@@ -184,16 +210,16 @@
     arrive(fx)
 
     def kv_part(b):
-        return mm(fg[b][:, : 8 * KA], wa[b].reshape(8 * KA, 2 * HC))
-
-    kv[...] = kv_part(y)
+        return mm(fg[b], wa[b].reshape(8 * RK, 256))
+
+    kv[:, 0:256] = kv_part(y)
     for step in (2, 3, 4):
         arrive(ra)
         ra = a2(step)
         arrive(rb)
         rb = b2(step)
-        kv[...] += kv_part((y - fwd * (step - 1) + 16) % 8)
-        kv[...] += kv_part((y + fwd * (step - 1) + 16) % 8)
+        kv[:, 0:256] += kv_part((y - fwd * (step - 1) + 16) % 8)
+        kv[:, 0:256] += kv_part((y + fwd * (step - 1) + 16) % 8)
         if step == 2:
             ex = along_x_forward(ex, e_half, e_whole)
             dx = along_x_start(dec_in, lambda h: dec_in.at[:, pl.ds(32 * h, 32)], d_half, d_whole)
@@ -201,13 +227,17 @@
             ex = along_x_last(ex, e_half, e_whole)
     arrive(ra)
     arrive(rb)
-    kv[...] += kv_part((y + 4) % 8)
-    for b in range(8):
-        kv[...] += mm(fg[b][:, 8 * KA :], wb[:, b, 0:16, :].reshape(128, 2 * HC))
+    kv[:, 0:256] += kv_part((y + 4) % 8)
+
+    def kv_rest(b, total):
+        return total + mm(fg[b], wb[:, b, 0:RK, :].reshape(8 * RK, 128))
+
+    kv[:, 256:384] = lax.fori_loop(0, 8, kv_rest, jnp.zeros((GROUP * CTX, 128), F32))
 
     def unpack(zz, carry):
         for yy in range(NY):
-            qo[yy * NZ + zz] = wb[zz, yy, 16:40, :].astype(F32)
+            tiles = wb[zz, yy, RK:RB, :].astype(F32)
+            qo[yy * NZ + zz] = jnp.concatenate([tiles[24 * r : 24 * r + 24] for r in range(3)], axis=1)
         return carry
 
     lax.fori_loop(0, NZ, unpack, 0)
@@ -215,7 +245,7 @@
     def split(b, carry):
         rows = qo[pl.ds(8 * b, 8)].reshape(HC, 2 * HC)
         wq[pl.ds(pl.multiple_of(HC * b, HC), HC), :] = rows[:, :HC].astype(BF)
-        wo[pl.ds(pl.multiple_of(HC * b, HC), HC), :] = rows[:, HC:].astype(BF)
+        wo[pl.ds(pl.multiple_of(HC * b, HC), HC), :] = jnp.concatenate([rows[:, 256:], rows[:, HC:256]], axis=1).astype(BF)
         return carry
 
     lax.fori_loop(0, NY, split, 0)
@@ -242,7 +272,6 @@
 
     arrive(ex)
     dx = along_x_forward(dx, d_half, d_whole)
-    lane = lax.broadcasted_iota(jnp.int32, (STEPS, 2 * STEPS), 1)
     scale = 1.0 / math.sqrt(HD)
 
     def two_spans(pair):
@@ -295,16 +324,17 @@
     predicted = ps[j].astype(F32)
     for k in range(1, ne):
         predicted += pr[k - 1].astype(F32)
-    length, dims = meta_in[0:1, :], meta_in[1:2, :]
+    low_lane = lane[0:1] < STEPS
+    length = jnp.where(low_lane, lengths[0].astype(F32), lengths[1].astype(F32))
+    dims = jnp.where(low_lane, act_dims[emb_ids[0]].astype(F32), act_dims[emb_ids[1]].astype(F32))
     step_row = lax.broadcasted_iota(jnp.int32, (STEPS, 2 * STEPS), 0).astype(F32)
     step_col = (lane & (STEPS - 1)).astype(F32)
     valid = jnp.where((step_row < length) & (step_col < dims), 1.0, 0.0).astype(F32)
     error = predicted - vel_in[...]
     squares = jnp.sum(valid * error * error, axis=0, keepdims=True)
-    low_lane = lane[0:1] < STEPS
-    for q in range(2):
-        one = jnp.sum(jnp.where(low_lane == (q == 0), squares, 0.0), axis=1, keepdims=True)
-        loss_out[q : q + 1, :] = one / length[:, 64 * q : 64 * q + 1] + jnp.zeros((1, 128), F32)
+    sums = [jnp.sum(jnp.where(half_lanes, squares, 0.0), axis=1, keepdims=True) for half_lanes in (low_lane, ~low_lane)]
+    one = [sums[q] / jnp.full((1, 1), lengths[q].astype(F32), F32) for q in range(2)]
+    loss_out[...] = jnp.where(id_lane == 0, one[0], one[1])
     dp_own[...] = (2.0 * valid * error / length).astype(BF)
     errors = [go(dp_own, dpg.at[j], dev_e((j + k) % ne)) for k in range(1, ne)]
     dpg[j] = dp_own[...]
@@ -380,57 +410,37 @@
     gq_copies = finish(0, gq_copies, z, dev_z)
     go_copies = gather(1, go_copies, z, dev_z)
     gq_copies = gather(0, gq_copies, y, dev_y)
-    arrive(go_copies)
-    go_out[...] = og[1].reshape(8, 96, 384)
-    arrive(gq_copies)
-    gq_out[...] = og[0].reshape(8, 96, 384)
+    for n, copies, out in ((1, go_copies, go_out), (0, gq_copies, gq_out)):
+        arrive(copies)
+        for t in range(8):
+            rows, columns = 96 * (t // 4), 384 * (t % 4)
+            out[rows : rows + 96, columns : columns + 384] = og[n, t].reshape(96, 384)
     for copy in cs.made:
         copy.wait_send()
 
 
-def step_embedding(step_values, width):
-    half = width // 2
-    freq = jnp.exp(-math.log(10000.0) * jnp.arange(half, dtype=F32) / half)
-    angle = step_values.astype(F32)[:, None] * freq[None, :]
-    return jnp.concatenate([jnp.sin(angle), jnp.cos(angle)], axis=1)
-
-
-def side_by_side(spans):
-    return jnp.concatenate([spans[0], spans[1]], axis=1)
-
-
 def body(actions, noise, emb_ids, lengths, t_index, act_dims, features, enc_w, dec_w, wq, wk, wv, wo_t):
-    shard = jnp.concatenate(
-        [jnp.concatenate([wk, wv], axis=1), jnp.concatenate([wq, wo_t], axis=1), jnp.zeros((8, 2 * HC), BF)], axis=0
-    )
-    flat = features.reshape(GROUP * CTX, 8, 80)
-    feats = jnp.concatenate(
-        [flat[:, :, :KA].reshape(GROUP * CTX, 8 * KA), flat[:, :, KA:].reshape(GROUP * CTX, 128)], axis=1
-    )
-    act, noi = actions.astype(F32), noise.astype(F32)
-    fraction = (t_index.astype(F32) / TSTEPS)[:, None, None]
-    noisy = side_by_side(((1.0 - fraction) * noi + fraction * act).astype(BF))
-    velocity = side_by_side(act - noi)
-    code = step_embedding(t_index, H).reshape(8, 384)
-    dims = act_dims[emb_ids]
-    meta = jnp.stack(
-        [jnp.repeat(lengths, STEPS).astype(F32), jnp.repeat(dims, STEPS).astype(F32)] + [jnp.ones((128,), F32)] * 6
-    )
-    ids = jnp.zeros((8, 128), jnp.int32).at[0, 0:2].set(emb_ids)
     vm = pl.BlockSpec(memory_space=pltpu.VMEM)
+    sm = pl.BlockSpec(memory_space=pltpu.SMEM)
     V = pltpu.VMEM
     d_q, d_o, loss = pl.pallas_call(
         kernel,
         out_shape=(
-            jax.ShapeDtypeStruct((8, 96, 384), BF),
-            jax.ShapeDtypeStruct((8, 96, 384), BF),
+            jax.ShapeDtypeStruct((HC, H), BF),
+            jax.ShapeDtypeStruct((HC, H), BF),
             jax.ShapeDtypeStruct((8, 128), F32),
         ),
-        in_specs=[vm] * 10,
+        in_specs=[vm] * 2 + [sm] * 4 + [vm] * 7,
         out_specs=(vm, vm, vm),
         scratch_shapes=[
-            V((NY, NZ, KA, 2 * HC), BF),
-            V((NZ, NY, KB, 2 * HC), BF),
+            V((RK, 256), BF),
+            V((RB, 128), BF),
+            V((STEPS, 128), BF),
+            V((STEPS, 128), F32),
+            V((8, 384), F32),
+            V((8, 128), jnp.int32),
+            V((NY, NZ, RK, 256), BF),
+            V((NZ, NY, RB, 128), BF),
             V((8, GROUP * CTX, 640), BF),
             V((EMBS, STEPS, H), BF),
             V((EMBS, STEPS, H), BF),
@@ -468,12 +478,11 @@
         compiler_params=pltpu.CompilerParams(
             collective_id=0, has_side_effects=True, vmem_limit_bytes=56 * 1024 * 1024
         ),
-    )(shard[:KA], shard[KA:], feats, enc_w, jnp.swapaxes(dec_w, 1, 2), noisy, velocity, meta, code, ids)
-
-    def whole(slices):
-        return slices.astype(F32).reshape(2, 4, 96, 384).transpose(0, 2, 1, 3).reshape(HC, H)
-
-    return whole(d_q), whole(d_o), loss[0:2, 0]
+    )(
+        actions, noise, emb_ids, lengths, t_index, act_dims, features.reshape(GROUP * CTX, 640), enc_w,
+        jnp.swapaxes(dec_w, 1, 2), wq, wk, wv, wo_t,
+    )
+    return d_q.astype(F32), d_o.astype(F32), loss[0, 0:2]
 
 
 def solution(mesh):

time: 168 us -> 152 us (0.905)
  local copies, waits for them, and re-layouts: 9.22 us -> 1.25 us
  other arithmetic: 10.6 us -> 3.35 us
    concatenate x6 -> x0, other arithmetic: 4.97 us -> none  [the longest x1 1.47 us: body(): jnp.concatenate([wk, wv], axis=1)]
    reshape x6 -> x0, local copies, waits for them, and re-layouts: 2.63 us -> none  [the longest x2 1.52 us: whole(): slices.astype(F32).reshape(2, 4, 96, 384).transpose(0, 2, 1, 3)]
    unnamed x8 -> x2, local copies, waits for them, and re-layouts: 2.33 us -> 0.01 us
    convert_element_type x3 -> x2, other arithmetic: 1.36 us -> 3.35 us  [body(): return (d_q.astype(F32), d_o.astype(F32), loss[0, 0:2])]
    slice x5 -> x0, local copies, waits for them, and re-layouts: 1.89 us -> none  [the longest x1 1.3 us: body(): return (whole(d_q), whole(d_o), loss[0:2, 0])]
where the time goes in v2:
time: 152 us
  Pallas kernels  147 us (97%)
  other arithmetic  3.35 us (2%)
    pallas_call x1, Pallas kernels, body(): pl.pallas_call(kernel, out_shape=(jax.ShapeDtypeStruct((HC, H), BF), jax....  147 us
    convert_element_type x2, other arithmetic, body(): return (d_q.astype(F32), d_o.astype(F32), loss[0, 0:2])  3.35 us

profile of v2, /device:TPU:16, one launch (start us, length us, event | category | flops | bytes accessed | tf_op | source)
XLA Modules:
  0.0 151.8 jit_solution(6555846560239897361)
XLA Ops:
  0.6 146.6 %shard_map.148 = (bf16[192,1536]{1,0:T(8,128)(2,1)}, bf16[192,1536]{1,0:T(8,128)(2,1)}, f32[8,128]{1,0:T(8,128)}) custom-call(bf16[2,64,64]{2,1,0:T(8,128)(2,1)} %act.1, bf16[2,64,64]{2,1,0:T(8,128)(2,1)} %noise.1, s32[2]{0:T(128)} %emb_ids.1, s32[2]{0:T(128)} %lengths.1, s32[2]{0:T(128)} %levels.1, s32[24]{0:T(128)} %act_dims.1, bf16[128,640]{1,0:T(8,128)(2,1)} %bitcast.5, ...), custom_call_target="tpu_custom_call" | custom-call | tf_op jit(solution)/shard_map/pallas_call | solution.py:426
  147.2 0.0 copy-start
  147.2 1.2 slice_bitcast_fusion
  148.5 2.2 %convert_element_type.6 = f32[192,1536]{1,0:T(8,128)} convert(bf16[192,1536]{1,0:T(8,128)(2,1)} %get-tuple-element.6) | non-fusion elementwise | flops 294912 | bytes 1769472 | tf_op jit(solution)/shard_map/convert_element_type | solution.py:485
  150.7 0.0 copy-done
  150.7 1.1 convert_element_type.7
Async XLA Ops:
  147.2 3.5 %copy-start = (bf16[192,1536]{1,0:T(8,128)(2,1)S(1)}, bf16[192,1536]{1,0:T(8,128)(2,1)}, u32[]{:S(2)}) copy-start(bf16[192,1536]{1,0:T(8,128)(2,1)} %get-tuple-element.7) | copy-start | bytes 1769476

commit v3 on v2

--- a/solution.py
+++ b/solution.py
@@ -61,7 +61,7 @@
     wa_in, wb_in, nz_in, vel_in, code_in, ids_in,
     wa, wb, fg, eg, dg, nzg, cg, ig, ids, kv, qo, wq, wo, kb, vb,
     hid, dbr, prs, att, att_t, dq_t, ps, pr, dp_own, dpg,
-    gs, gr, sb, sr, fs, sg, og, send_sems, recv_sems, local_sem,
+    gs, own_slice, gr, sb, sr, fs, sg, og, send_sems, recv_sems, local_sem,
 ):
     i = lax.axis_index("dp")
     j = lax.axis_index("emb")
@@ -117,28 +117,37 @@
         small.append(go(code_in, cg.at[j], peer))
         small.append(go(ids_in, ig.at[j], peer))
 
-    def ring(step, me, device, first, block, heavy, light):
-        up = device((me + fwd + 8) % 8)
-        down = device((me - fwd + 8) % 8)
-        out = []
-        if step <= heavy:
-            b = (me - fwd * (step - 1) + 16) % 8
-            for src, dst in zip(first if step == 1 and first else block(b), block(b)):
-                out.append(go(src, dst, up))
-        if step <= light:
-            b = (me + fwd * (step - 1) + 16) % 8
-            for src, dst in zip(first if step == 1 and first else block(b), block(b)):
-                out.append(go(src, dst, down))
-        return out
-
     def arrive(copies):
         for copy in copies:
             copy.wait_recv()
 
-    a1 = lambda s: ring(s, z, dev_z, [wa_in], lambda b: [wa.at[y, b]], 4, 3)
-    b1 = lambda s: ring(s, y, dev_y, [wb_in], lambda b: [wb.at[z, b]], 4, 3)
-    a2 = lambda s: ring(s, y, dev_y, None, lambda b: [wa.at[b, pl.ds(0, 4)], wa.at[b, pl.ds(4, 4)]], 4, 3)
-    b2 = lambda s: ring(s, z, dev_z, None, lambda b: [wb.at[b, pl.ds(0, 4)], wb.at[b, pl.ds(4, 4)]], 4, 3)
+    def first_ring(step, me, device, own, slot):
+        out = [go(own if step == 1 else slot(2 * step - 3), slot(2 * step - 1), device((me + fwd + 8) % 8))]
+        if step <= 3:
+            out.append(go(own if step == 1 else slot(2 * step - 2), slot(2 * step), device((me - fwd + 8) % 8)))
+        return out
+
+    pieces = ((0, 3), (3, 2), (5, 3))
+
+    def second_ring(step, piece, me, device, buf):
+        start, size = pieces[piece]
+        b = (me - fwd * (step - 1) + 16) % 8
+        block = buf.at[b, pl.ds(start, size)]
+        out = [go(block, block, device((me + fwd + 8) % 8))]
+        if step <= 3:
+            b = (me + fwd * (step - 1) + 16) % 8
+            block = buf.at[b, pl.ds(start, size)]
+            out.append(go(block, block, device((me - fwd + 8) % 8)))
+        return out
+
+    def place_of(t, me):
+        away = ((t - me) * fwd + 8) % 8
+        return 2 * away - (away // 4) * (4 * away - 15)
+
+    a1 = lambda s: first_ring(s, z, dev_z, wa_in, lambda p: wa.at[y, p])
+    b1 = lambda s: first_ring(s, y, dev_y, wb_in, lambda p: wb.at[z, p])
+    a2 = lambda s, p: second_ring(s, p, y, dev_y, wa)
+    b2 = lambda s, p: second_ring(s, p, z, dev_z, wb)
 
     right, left = (2 * ((x + 1) % NX) + c), (2 * ((x + 3) % NX) + c)
     opposite, sibling = (2 * ((x + 2) % NX) + c), (2 * x + 1 - c)
@@ -183,8 +192,8 @@
     fx = along_x_start(f_in, lambda h: f_in.at[pl.ds(64 * h, 64)], f_half, f_whole)
     ex = along_x_start(enc_in, lambda h: enc_in.at[:, pl.ds(32 * h, 32)], e_half, e_whole)
 
-    wa[y, z] = wa_in[...]
-    wb[z, y] = wb_in[...]
+    wa[y, 0] = wa_in[...]
+    wb[z, 0] = wb_in[...]
     fg[j] = f_in[...]
     eg[pl.ds(3 * j, 3)] = enc_in[...]
     dg[pl.ds(3 * j, 3)] = dec_in[...]
@@ -192,16 +201,16 @@
     cg[j] = code_in[...]
     ig[j] = ids_in[...]
 
-    for step in (2, 3, 4):
+    ring = []
+    for step in (1, 2, 3, 4):
         arrive(ra)
-        ra = a1(step)
         arrive(rb)
-        rb = b1(step)
+        if step < 4:
+            ra, rb = a1(step + 1), b1(step + 1)
+        if step != 3:
+            piece = len(ring)
+            ring.append((a2(1, piece), b2(1, piece)))
     fx = along_x_forward(fx, f_half, f_whole)
-    arrive(ra)
-    ra = a2(1)
-    arrive(rb)
-    rb = b2(1)
     fx = along_x_last(fx, f_half, f_whole)
     arrive(small)
     table = pltpu.make_async_copy(ig, ids, local_sem)
@@ -210,76 +219,10 @@
     arrive(fx)
 
     def kv_part(b):
-        return mm(fg[b], wa[b].reshape(8 * RK, 256))
+        rows = jnp.concatenate([wa[b, place_of(t, z)] for t in range(8)], axis=0)
+        return mm(fg[b], rows)
 
     kv[:, 0:256] = kv_part(y)
-    for step in (2, 3, 4):
-        arrive(ra)
-        ra = a2(step)
-        arrive(rb)
-        rb = b2(step)
-        kv[:, 0:256] += kv_part((y - fwd * (step - 1) + 16) % 8)
-        kv[:, 0:256] += kv_part((y + fwd * (step - 1) + 16) % 8)
-        if step == 2:
-            ex = along_x_forward(ex, e_half, e_whole)
-            dx = along_x_start(dec_in, lambda h: dec_in.at[:, pl.ds(32 * h, 32)], d_half, d_whole)
-        if step == 3:
-            ex = along_x_last(ex, e_half, e_whole)
-    arrive(ra)
-    arrive(rb)
-    kv[:, 0:256] += kv_part((y + 4) % 8)
-
-    def kv_rest(b, total):
-        return total + mm(fg[b], wb[:, b, 0:RK, :].reshape(8 * RK, 128))
-
-    kv[:, 256:384] = lax.fori_loop(0, 8, kv_rest, jnp.zeros((GROUP * CTX, 128), F32))
-
-    def unpack(zz, carry):
-        for yy in range(NY):
-            tiles = wb[zz, yy, RK:RB, :].astype(F32)
-            qo[yy * NZ + zz] = jnp.concatenate([tiles[24 * r : 24 * r + 24] for r in range(3)], axis=1)
-        return carry
-
-    lax.fori_loop(0, NZ, unpack, 0)
-
-    def split(b, carry):
-        rows = qo[pl.ds(8 * b, 8)].reshape(HC, 2 * HC)
-        wq[pl.ds(pl.multiple_of(HC * b, HC), HC), :] = rows[:, :HC].astype(BF)
-        wo[pl.ds(pl.multiple_of(HC * b, HC), HC), :] = jnp.concatenate([rows[:, 256:], rows[:, HC:256]], axis=1).astype(BF)
-        return carry
-
-    lax.fori_loop(0, NY, split, 0)
-
-    head_of_row = lax.broadcasted_iota(jnp.int32, (32, HC), 0) >> 3
-    column = lax.broadcasted_iota(jnp.int32, (32, HC), 1)
-    low = head_of_row * HD
-    head_mask = jnp.where((column >= low) & (column < low + HD), 1.0, 0.0).astype(F32)
-
-    def spread(flat):
-        three = flat.astype(BF).astype(F32).reshape(GROUP, CTX, HC)
-        return (jnp.concatenate([three] * 4, axis=1) * head_mask[None]).astype(BF)
-
-    kb[...] = spread(kv[:, :HC])
-    vb[...] = spread(kv[:, HC:])
-
-    same_head = jnp.where(
-        (lax.broadcasted_iota(jnp.int32, (32, 32), 0) >> 3)
-        == (lax.broadcasted_iota(jnp.int32, (32, 32), 1) >> 3), 1.0, 0.0,
-    ).astype(F32)
-
-    def head_sum(values):
-        return jnp.dot(values, same_head, precision=lax.Precision.HIGHEST, preferred_element_type=F32)
-
-    arrive(ex)
-    dx = along_x_forward(dx, d_half, d_whole)
-    scale = 1.0 / math.sqrt(HD)
-
-    def two_spans(pair):
-        zero = jnp.zeros_like(pair)
-        return jnp.concatenate([jnp.where(lane < STEPS, pair, zero), jnp.where(lane >= STEPS, pair, zero)], axis=0)
-
-    def weights_of(buf, p):
-        return jnp.concatenate([buf[ids[p, 0, 0]], buf[ids[p, 0, 1]]], axis=0)
 
     def encode(p, carry):
         enc = mm(two_spans(nzg[p]), weights_of(eg, p)).astype(BF).astype(F32)
@@ -289,7 +232,77 @@
             hid[pl.ds(pl.multiple_of(p * 128 + 64 * q, 64), 64), :] = (enc[64 * q : 64 * q + 64] + row).astype(BF)
         return carry
 
+    def two_spans(pair):
+        zero = jnp.zeros_like(pair)
+        return jnp.concatenate([jnp.where(lane < STEPS, pair, zero), jnp.where(lane >= STEPS, pair, zero)], axis=0)
+
+    def weights_of(buf, p):
+        return jnp.concatenate([buf[ids[p, 0, 0]], buf[ids[p, 0, 1]]], axis=0)
+
+    for step in (2, 3, 4):
+        later = []
+        for piece in range(3):
+            for copies in ring[piece]:
+                arrive(copies)
+            later.append((a2(step, piece), b2(step, piece)))
+        ring = later
+        if step == 2:
+            ex = along_x_forward(ex, e_half, e_whole)
+            dx = along_x_start(dec_in, lambda h: dec_in.at[:, pl.ds(32 * h, 32)], d_half, d_whole)
+        if step == 3:
+            ex = along_x_last(ex, e_half, e_whole)
+        kv[:, 0:256] += kv_part((y - fwd * (step - 1) + 16) % 8)
+        kv[:, 0:256] += kv_part((y + fwd * (step - 1) + 16) % 8)
+    arrive(ex)
     lax.fori_loop(0, ne, encode, 0)
+    for piece in range(3):
+        for copies in ring[piece]:
+            arrive(copies)
+    dx = along_x_forward(dx, d_half, d_whole)
+    kv[:, 0:256] += kv_part((y + 4) % 8)
+
+    def kv_rest(b, total):
+        return total + mm(fg[b], wb[:, place_of(b, y), 0:RK, :].reshape(8 * RK, 128))
+
+    kv[:, 256:384] = lax.fori_loop(0, 8, kv_rest, jnp.zeros((GROUP * CTX, 128), F32))
+
+    def unpack(zz, carry):
+        for yy in range(NY):
+            tiles = wb[zz, place_of(yy, y), RK:RB, :].astype(F32)
+            qo[yy * NZ + zz] = jnp.concatenate([tiles[24 * r : 24 * r + 24] for r in range(3)], axis=1)
+        return carry
+
+    lax.fori_loop(0, NZ, unpack, 0)
+
+    def split(b, carry):
+        rows = qo[pl.ds(8 * b, 8)].reshape(HC, 2 * HC)
+        wq[pl.ds(pl.multiple_of(HC * b, HC), HC), :] = rows[:, :HC].astype(BF)
+        wo[pl.ds(pl.multiple_of(HC * b, HC), HC), :] = jnp.concatenate([rows[:, 256:], rows[:, HC:256]], axis=1).astype(BF)
+        return carry
+
+    lax.fori_loop(0, NY, split, 0)
+
+    head_of_row = lax.broadcasted_iota(jnp.int32, (32, HC), 0) >> 3
+    column = lax.broadcasted_iota(jnp.int32, (32, HC), 1)
+    low = head_of_row * HD
+    head_mask = jnp.where((column >= low) & (column < low + HD), 1.0, 0.0).astype(F32)
+
+    def spread(flat):
+        three = flat.astype(BF).astype(F32).reshape(GROUP, CTX, HC)
+        return (jnp.concatenate([three] * 4, axis=1) * head_mask[None]).astype(BF)
+
+    kb[...] = spread(kv[:, :HC])
+    vb[...] = spread(kv[:, HC:])
+
+    same_head = jnp.where(
+        (lax.broadcasted_iota(jnp.int32, (32, 32), 0) >> 3)
+        == (lax.broadcasted_iota(jnp.int32, (32, 32), 1) >> 3), 1.0, 0.0,
+    ).astype(F32)
+
+    def head_sum(values):
+        return jnp.dot(values, same_head, precision=lax.Precision.HIGHEST, preferred_element_type=F32)
+
+    scale = 1.0 / math.sqrt(HD)
 
     def attend(g, carry):
         here = pl.ds(pl.multiple_of(256 * g, 256), 256)
@@ -347,20 +360,26 @@
 
     lax.fori_loop(0, ne, d_branch, 0)
 
-    def slice_of(left_t, right_rows, t):
-        rows = pl.ds(pl.multiple_of(96 * (t // 4), 16), 96)
-        columns = pl.ds(pl.multiple_of(384 * (t % 4), 128), 384)
-        return mm(left_t[rows, :], right_rows[:, columns])
-
-    def scatter(n, left_t, right_rows, me, device):
+    first_of = ((y, dev_y), (z, dev_z))
+
+    def scatter(n, left_t, right_rows):
         out = []
-        for k in range(1, 8):
-            t = (me + k) % 8
-            gs[n, k - 1] = slice_of(left_t, right_rows, t).astype(BF)
-            out.append(go(gs.at[n, k - 1], gr.at[n, k - 1], device(t)))
+        for h, (me, device) in enumerate(first_of):
+            for k in (1, 2, 3, 0):
+                columns = pl.ds(pl.multiple_of(384 * ((me + k) % 4), 128), 384)
+                part = mm(left_t[96 * h : 96 * h + 96, :], right_rows[:, columns])
+                gs[n, h, k] = part.astype(BF)
+                if k == 0:
+                    upper = jnp.where(me // 4 == 0, 1.0, 0.0).astype(F32)
+                    own_slice[n, h] = upper * part[0:48] + (1.0 - upper) * part[48:96]
+                for o in (k, k + 4):
+                    if o:
+                        t = (me + o) % 8
+                        rows = pl.ds(pl.multiple_of(48 * (t // 4), 16), 48)
+                        out.append(go(gs.at[n, h, k, rows], gr.at[n, h, o - 1], device(t)))
         return out
 
-    go_copies = scatter(1, att_t, dbr, z, dev_z)
+    go_copies = scatter(1, att_t, dbr)
 
     def back(g, carry):
         here = pl.ds(pl.multiple_of(256 * g, 256), 256)
@@ -373,50 +392,83 @@
         return carry
 
     lax.fori_loop(0, 4, back, 0)
-    gq_copies = scatter(0, dq_t, hid, y, dev_y)
-
-    def add_up(n, copies, left_t, right_rows, me, me2, device2):
-        total = slice_of(left_t, right_rows, me)
+    gq_copies = scatter(0, dq_t, hid)
+
+    def add_up(n, copies):
         arrive(copies)
-        for k in range(7):
-            total += gr[n, k].astype(F32)
-        sb[n, 0:96] = total.astype(BF)
-        sb[n, 96:128] = jnp.zeros((32, 384), BF)
         out = []
-        for k in range(1, 8):
-            t = (me2 + k) % 8
-            out.append(go(sb.at[n, pl.ds(pl.multiple_of(16 * t, 16), 16)], sr.at[n, k - 1], device2(t)))
+        for h in range(2):
+            total = own_slice[n, h]
+            for k in range(7):
+                total += gr[n, h, k].astype(F32)
+            for t in range(9):
+                sb[n, h, t] = total[16 * (t // 3) : 16 * (t // 3) + 16, 128 * (t % 3) : 128 * (t % 3) + 128].astype(BF)
+            me, device = first_of[1 - h]
+            for k in range(1, 8):
+                t = (me + k) % 8
+                out.append(go(sb.at[n, h, pl.ds(2 * t, 2)], sr.at[n, h, k - 1], device(t)))
         return out
 
-    def finish(n, copies, me2, device2):
+    def finish(n, copies):
         arrive(copies)
-        total = sb[n, pl.ds(pl.multiple_of(16 * me2, 16), 16)].astype(F32)
-        for k in range(7):
-            total += sr[n, k].astype(F32)
-        fs[n] = total.astype(BF)
-        out = [go(fs.at[n], sg.at[n, me2], device2((me2 + k) % 8)) for k in range(1, 8)]
-        sg[n, me2] = fs[n]
+        out = []
+        for h in range(2):
+            me, device = first_of[1 - h]
+            total = sb[n, h, pl.ds(2 * me, 2)].astype(F32)
+            for k in range(7):
+                total += sr[n, h, k].astype(F32)
+            fs[n, h] = total.astype(BF)
+            out += [go(fs.at[n, h], sg.at[n, h, pl.ds(2 * me, 2)], device((me + k) % 8)) for k in range(1, 8)]
+            sg[n, h, pl.ds(2 * me, 2)] = fs[n, h]
         return out
 
-    def gather(n, copies, me, device):
+    def gather(n, step, copies):
         arrive(copies)
-        out = [go(sg.at[n, pl.ds(0, 6)], og.at[n, me], device((me + k) % 8)) for k in range(1, 8)]
-        og[n, me] = sg[n, 0:6]
+        out = []
+        for h, (me, device) in enumerate(first_of):
+            b = (me - fwd * (step - 1) + 16) % 8
+            first = sg.at[n, h, pl.ds(0, 9)]
+            out.append(go(first if step == 1 else og.at[n, h, b], og.at[n, h, b], device((me + fwd + 8) % 8)))
+            if step <= 3:
+                b = (me + fwd * (step - 1) + 16) % 8
+                out.append(go(first if step == 1 else og.at[n, h, b], og.at[n, h, b], device((me - fwd + 8) % 8)))
+            if step == 1:
+                og[n, h, me] = sg[n, h, 0:9]
         return out
 
-    go_copies = add_up(1, go_copies, att_t, dbr, z, y, dev_y)
-    gq_copies = add_up(0, gq_copies, dq_t, hid, y, z, dev_z)
-    go_copies = finish(1, go_copies, y, dev_y)
-    gq_copies = finish(0, gq_copies, z, dev_z)
-    go_copies = gather(1, go_copies, z, dev_z)
-    gq_copies = gather(0, gq_copies, y, dev_y)
-    for n, copies, out in ((1, go_copies, go_out), (0, gq_copies, gq_out)):
-        arrive(copies)
-        for t in range(8):
-            rows, columns = 96 * (t // 4), 384 * (t % 4)
-            out[rows : rows + 96, columns : columns + 384] = og[n, t].reshape(96, 384)
+    def write(n, out):
+        for h in range(2):
+            for t in range(8):
+                for r in range(9):
+                    row, column = 96 * h + 48 * (t // 4) + 16 * (r // 3), 384 * (t % 4) + 128 * (r % 3)
+                    out[row : row + 16, column : column + 128] = og[n, h, t, r]
+
+    sb[:, :, 9:16] = jnp.zeros((2, 2, 7, 16, 128), BF)
+    go_copies = add_up(1, go_copies)
+    go_copies = finish(1, go_copies)
+    gq_copies = add_up(0, gq_copies)
+    go_copies = gather(1, 1, go_copies)
+    gq_copies = finish(0, gq_copies)
+    go_copies = gather(1, 2, go_copies)
+    gq_copies = gather(0, 1, gq_copies)
+    go_copies = gather(1, 3, go_copies)
+    gq_copies = gather(0, 2, gq_copies)
+    go_copies = gather(1, 4, go_copies)
+    gq_copies = gather(0, 3, gq_copies)
+    arrive(go_copies)
+    gq_copies = gather(0, 4, gq_copies)
+    write(1, go_out)
+    arrive(gq_copies)
+    write(0, gq_out)
     for copy in cs.made:
         copy.wait_send()
+
+
+def widen(q_in, o_in, loss_in, q_out, o_out, loss_out):
+    q_out[...] = q_in[...].astype(F32)
+    o_out[...] = o_in[...].astype(F32)
+    for q in range(2):
+        loss_out[q] = loss_in[0, q]
 
 
 def body(actions, noise, emb_ids, lengths, t_index, act_dims, features, enc_w, dec_w, wq, wk, wv, wo_t):
@@ -464,13 +516,14 @@
             V((7, STEPS, 128), BF),
             V((STEPS, 128), BF),
             V((8, STEPS, 128), BF),
-            V((2, 7, 96, 384), BF),
-            V((2, 7, 96, 384), BF),
-            V((2, 128, 384), BF),
-            V((2, 7, 16, 384), BF),
-            V((2, 16, 384), BF),
-            V((2, 8, 16, 384), BF),
-            V((2, 8, 6, 16, 384), BF),
+            V((2, 2, 4, 96, 384), BF),
+            V((2, 2, 48, 384), F32),
+            V((2, 2, 7, 48, 384), BF),
+            V((2, 2, 16, 16, 128), BF),
+            V((2, 2, 7, 2, 16, 128), BF),
+            V((2, 2, 2, 16, 128), BF),
+            V((2, 2, 16, 16, 128), BF),
+            V((2, 2, 8, 9, 16, 128), BF),
             pltpu.SemaphoreType.DMA((N_COPIES,)),
             pltpu.SemaphoreType.DMA((N_COPIES,)),
             pltpu.SemaphoreType.DMA,
@@ -482,7 +535,14 @@
         actions, noise, emb_ids, lengths, t_index, act_dims, features.reshape(GROUP * CTX, 640), enc_w,
         jnp.swapaxes(dec_w, 1, 2), wq, wk, wv, wo_t,
     )
-    return d_q.astype(F32), d_o.astype(F32), loss[0, 0:2]
+    return pl.pallas_call(
+        widen,
+        out_shape=(
+            jax.ShapeDtypeStruct((HC, H), F32), jax.ShapeDtypeStruct((HC, H), F32), jax.ShapeDtypeStruct((2,), F32),
+        ),
+        in_specs=[vm, vm, sm],
+        out_specs=(vm, vm, sm),
+    )(d_q, d_o, loss)
 
 
 def solution(mesh):

time: 152 us -> 141 us (0.928)
  the two profiles are of different devices: /device:TPU:16 before, /device:TPU:6 now
where the time goes in v3:
time: 141 us
  Pallas kernels  140 us (99%)
    pallas_call x1, Pallas kernels, body(): pl.pallas_call(kernel, out_shape=(jax.ShapeDtypeStruct((HC, H), BF), jax....  138 us

profile of v3, /device:TPU:6, one launch (start us, length us, event | category | flops | bytes accessed | tf_op | source)
XLA Modules:
  0.0 141.0 jit_solution(15533234571168564707)
XLA Ops:
  0.6 137.6 %shard_map.148 = (bf16[192,1536]{1,0:T(8,128)(2,1)}, bf16[192,1536]{1,0:T(8,128)(2,1)}, f32[8,128]{1,0:T(8,128)}) custom-call(bf16[2,64,64]{2,1,0:T(8,128)(2,1)} %act.1, bf16[2,64,64]{2,1,0:T(8,128)(2,1)} %noise.1, s32[2]{0:T(128)} %emb_ids.1, s32[2]{0:T(128)} %lengths.1, s32[2]{0:T(128)} %levels.1, s32[24]{0:T(128)} %act_dims.1, bf16[128,640]{1,0:T(8,128)(2,1)} %bitcast.3, ...), custom_call_target="tpu_custom_call" | custom-call | tf_op jit(solution)/shard_map/pallas_call | solution.py:478
  138.2 2.7 %shard_map.149 = (f32[192,1536]{1,0:T(8,128)}, f32[192,1536]{1,0:T(8,128)}, f32[2]{0:T(128)}) custom-call(bf16[192,1536]{1,0:T(8,128)(2,1)} %get-tuple-element.6.q_in, bf16[192,1536]{1,0:T(8,128)(2,1)} %get-tuple-element.7.o_in, f32[8,128]{1,0:T(8,128)} %get-tuple-element.8.loss_in), custom_call_target="tpu_custom_call" | custom-call | tf_op jit(solution)/shard_map/pallas_call | solution.py:538

commit v4 on v3

--- a/solution.py
+++ b/solution.py
@@ -61,7 +61,7 @@
     wa_in, wb_in, nz_in, vel_in, code_in, ids_in,
     wa, wb, fg, eg, dg, nzg, cg, ig, ids, kv, qo, wq, wo, kb, vb,
     hid, dbr, prs, att, att_t, dq_t, ps, pr, dp_own, dpg,
-    gs, own_slice, gr, sb, sr, fs, sg, og, send_sems, recv_sems, local_sem,
+    gs, wide, own_slice, gr, sb, sr, fs, sg, og, send_sems, recv_sems, local_sem,
 ):
     i = lax.axis_index("dp")
     j = lax.axis_index("emb")
@@ -166,6 +166,10 @@
         f0 = go(half(left, 0), half(left, 0), dev_e(right))
         l1.wait_recv()
         f1 = go(half(right, 1), half(right, 1), dev_e(left))
+        return f0, f1, r1, l0, s
+
+    def along_x_across(second, whole):
+        f0, f1, r1, l0, s = second
         r1.wait_recv()
         s0 = go(whole(left), whole(left), dev_e(sibling))
         l0.wait_recv()
@@ -211,18 +215,10 @@
             piece = len(ring)
             ring.append((a2(1, piece), b2(1, piece)))
     fx = along_x_forward(fx, f_half, f_whole)
-    fx = along_x_last(fx, f_half, f_whole)
-    arrive(small)
-    table = pltpu.make_async_copy(ig, ids, local_sem)
-    table.start()
-    table.wait()
-    arrive(fx)
 
     def kv_part(b):
         rows = jnp.concatenate([wa[b, place_of(t, z)] for t in range(8)], axis=0)
         return mm(fg[b], rows)
-
-    kv[:, 0:256] = kv_part(y)
 
     def encode(p, carry):
         enc = mm(two_spans(nzg[p]), weights_of(eg, p)).astype(BF).astype(F32)
@@ -247,18 +243,28 @@
             later.append((a2(step, piece), b2(step, piece)))
         ring = later
         if step == 2:
+            fx = along_x_across(fx, f_whole)
             ex = along_x_forward(ex, e_half, e_whole)
             dx = along_x_start(dec_in, lambda h: dec_in.at[:, pl.ds(32 * h, 32)], d_half, d_whole)
         if step == 3:
-            ex = along_x_last(ex, e_half, e_whole)
-        kv[:, 0:256] += kv_part((y - fwd * (step - 1) + 16) % 8)
-        kv[:, 0:256] += kv_part((y + fwd * (step - 1) + 16) % 8)
+            fx = along_x_last(fx, f_half, f_whole)
+            ex = along_x_across(ex, e_whole)
+    arrive(small)
+    table = pltpu.make_async_copy(ig, ids, local_sem)
+    table.start()
+    table.wait()
+    arrive(fx)
+    kv[:, 0:256] = kv_part(y)
+    for step in (1, 2, 3):
+        kv[:, 0:256] += kv_part((y - fwd * step + 16) % 8) + kv_part((y + fwd * step + 16) % 8)
+    ex = along_x_last(ex, e_half, e_whole)
     arrive(ex)
     lax.fori_loop(0, ne, encode, 0)
+    dx = along_x_forward(dx, d_half, d_whole)
     for piece in range(3):
         for copies in ring[piece]:
             arrive(copies)
-    dx = along_x_forward(dx, d_half, d_whole)
+    dx = along_x_across(dx, d_whole)
     kv[:, 0:256] += kv_part((y + 4) % 8)
 
     def kv_rest(b, total):
@@ -317,22 +323,30 @@
         att_t[:, here] = out.T.astype(BF)
         return carry
 
-    lax.fori_loop(0, 4, attend, 0)
+    lax.fori_loop(0, 3, attend, 0)
     dx = along_x_last(dx, d_half, d_whole)
+    lax.fori_loop(3, 4, attend, 0)
     arrive(dx)
 
-    def decode(p, carry):
-        here = pl.ds(pl.multiple_of(128 * p, 128), 128)
-        own = jnp.where(p == j, 1.0, 0.0).astype(F32)
-        branch = (mm_nt(att[here, :], wo[...]) + own * hid[here, :].astype(F32)).astype(BF)
-        ps[p] = jnp.concatenate(
-            [mm_nt(branch[64 * q : 64 * q + 64], dg[ids[p, 0, q]]) for q in range(2)], axis=1
-        ).astype(BF)
-        return carry
-
-    lax.fori_loop(0, ne, decode, 0)
-
-    shares = [go(ps.at[(j + k) % ne], pr.at[k - 1], dev_e((j + k) % ne)) for k in range(1, ne)]
+    def four_decoders(g):
+        return jnp.concatenate([weights_of(dg, 2 * g), weights_of(dg, 2 * g + 1)], axis=0)
+
+    shares = []
+    for k in (1, 2, 3, 0):
+        g = (x + k) % NX
+        here = pl.ds(pl.multiple_of(256 * g, 256), 256)
+        branch = mm_nt(att[here, :], wo[...])
+        if k == 0:
+            row_pair = lax.broadcasted_iota(jnp.int32, (256, H), 0) >> 7
+            branch += jnp.where(row_pair == c, hid[here, :].astype(F32), 0.0)
+        product = mm_nt(branch.astype(BF), four_decoders(g))
+        for r in range(2):
+            block = product[128 * r : 128 * r + 128, 128 * r : 128 * r + 128]
+            ps[2 * g + r] = jnp.where(lane < STEPS, block[0:STEPS], block[STEPS : 2 * STEPS]).astype(BF)
+        for r in range(2):
+            if k or r:
+                p = 2 * g + (c + r) % 2
+                shares.append(go(ps.at[p], pr.at[len(shares)], dev_e(p)))
     arrive(shares)
     predicted = ps[j].astype(F32)
     for k in range(1, ne):
@@ -353,30 +367,32 @@
     dpg[j] = dp_own[...]
     arrive(errors)
 
-    def d_branch(p, carry):
-        here = pl.ds(pl.multiple_of(128 * p, 128), 128)
-        dbr[here, :] = mm(two_spans(dpg[p]), weights_of(dg, p)).astype(BF)
+    def d_branch(g, carry):
+        upper, lower = two_spans(dpg[2 * g]), two_spans(dpg[2 * g + 1])
+        zero = jnp.zeros_like(upper)
+        left_rows = jnp.concatenate(
+            [jnp.concatenate([upper, zero], axis=1), jnp.concatenate([zero, lower], axis=1)], axis=0
+        )
+        dbr[pl.ds(pl.multiple_of(256 * g, 256), 256), :] = mm(left_rows, four_decoders(g)).astype(BF)
         return carry
 
-    lax.fori_loop(0, ne, d_branch, 0)
+    lax.fori_loop(0, 4, d_branch, 0)
 
     first_of = ((y, dev_y), (z, dev_z))
 
     def scatter(n, left_t, right_rows):
+        for q in range(4):
+            part = mm(left_t[...], right_rows[:, 384 * q : 384 * q + 384])
+            wide[q] = part
+            gs[n, q] = part.astype(BF)
         out = []
+        for k in (4, 3, 5, 2, 6, 1, 7):
+            for h, (me, device) in enumerate(first_of):
+                t = (me + k) % 8
+                rows = pl.ds(pl.multiple_of(96 * h + 48 * (t // 4), 16), 48)
+                out.append(go(gs.at[n, t % 4, rows], gr.at[n, h, k - 1], device(t)))
         for h, (me, device) in enumerate(first_of):
-            for k in (1, 2, 3, 0):
-                columns = pl.ds(pl.multiple_of(384 * ((me + k) % 4), 128), 384)
-                part = mm(left_t[96 * h : 96 * h + 96, :], right_rows[:, columns])
-                gs[n, h, k] = part.astype(BF)
-                if k == 0:
-                    upper = jnp.where(me // 4 == 0, 1.0, 0.0).astype(F32)
-                    own_slice[n, h] = upper * part[0:48] + (1.0 - upper) * part[48:96]
-                for o in (k, k + 4):
-                    if o:
-                        t = (me + o) % 8
-                        rows = pl.ds(pl.multiple_of(48 * (t // 4), 16), 48)
-                        out.append(go(gs.at[n, h, k, rows], gr.at[n, h, o - 1], device(t)))
+            own_slice[n, h] = wide[me % 4, pl.ds(pl.multiple_of(96 * h + 48 * (me // 4), 16), 48), :]
         return out
 
     go_copies = scatter(1, att_t, dbr)
@@ -516,7 +532,8 @@
             V((7, STEPS, 128), BF),
             V((STEPS, 128), BF),
             V((8, STEPS, 128), BF),
-            V((2, 2, 4, 96, 384), BF),
+            V((2, 4, HC, 384), BF),
+            V((4, HC, 384), F32),
             V((2, 2, 48, 384), F32),
             V((2, 2, 7, 48, 384), BF),
             V((2, 2, 16, 16, 128), BF),

time: 141 us -> 131 us (0.929)
  the two profiles are of different devices: /device:TPU:6 before, /device:TPU:64 now
where the time goes in v4:
time: 131 us
  Pallas kernels  130 us (99%)
    pallas_call x1, Pallas kernels, body(): pl.pallas_call(kernel, out_shape=(jax.ShapeDtypeStruct((HC, H), BF), jax....  127 us
    pallas_call x1, Pallas kernels, body(): pl.pallas_call(widen, out_shape=(jax.ShapeDtypeStruct((HC, H), F32), jax....  2.74 us

profile of v4, /device:TPU:64, one launch (start us, length us, event | category | flops | bytes accessed | tf_op | source)
XLA Modules:
  0.0 130.8 jit_solution(15011526263525936747)
XLA Ops:
  0.6 127.4 %shard_map.148 = (bf16[192,1536]{1,0:T(8,128)(2,1)}, bf16[192,1536]{1,0:T(8,128)(2,1)}, f32[8,128]{1,0:T(8,128)}) custom-call(bf16[2,64,64]{2,1,0:T(8,128)(2,1)} %act.1, bf16[2,64,64]{2,1,0:T(8,128)(2,1)} %noise.1, s32[2]{0:T(128)} %emb_ids.1, s32[2]{0:T(128)} %lengths.1, s32[2]{0:T(128)} %levels.1, s32[24]{0:T(128)} %act_dims.1, bf16[128,640]{1,0:T(8,128)(2,1)} %bitcast.3, ...), custom_call_target="tpu_custom_call" | custom-call | tf_op jit(solution)/shard_map/pallas_call | solution.py:494
  128.0 2.7 %shard_map.149 = (f32[192,1536]{1,0:T(8,128)}, f32[192,1536]{1,0:T(8,128)}, f32[2]{0:T(128)}) custom-call(bf16[192,1536]{1,0:T(8,128)(2,1)} %get-tuple-element.6.q_in, bf16[192,1536]{1,0:T(8,128)(2,1)} %get-tuple-element.7.o_in, f32[8,128]{1,0:T(8,128)} %get-tuple-element.8.loss_in), custom_call_target="tpu_custom_call" | custom-call | tf_op jit(solution)/shard_map/pallas_call | solution.py:555

commit v5 on v4

--- a/solution.py
+++ b/solution.py
@@ -301,9 +301,15 @@
     vb[...] = spread(kv[:, HC:])
 
     same_head = jnp.where(
-        (lax.broadcasted_iota(jnp.int32, (32, 32), 0) >> 3)
-        == (lax.broadcasted_iota(jnp.int32, (32, 32), 1) >> 3), 1.0, 0.0,
+        (lax.broadcasted_iota(jnp.int32, (128, 128), 0) >> 3)
+        == (lax.broadcasted_iota(jnp.int32, (128, 128), 1) >> 3), 1.0, 0.0,
     ).astype(F32)
+    same_span = (lax.broadcasted_iota(jnp.int32, (256, 128), 0) >> 6) == (
+        lax.broadcasted_iota(jnp.int32, (256, 128), 1) >> 5
+    )
+
+    def four(buf, g):
+        return buf[pl.ds(4 * g, 4)].reshape(128, HC)
 
     def head_sum(values):
         return jnp.dot(values, same_head, precision=lax.Precision.HIGHEST, preferred_element_type=F32)
@@ -313,12 +319,11 @@
     def attend(g, carry):
         here = pl.ds(pl.multiple_of(256 * g, 256), 256)
         queries = mm(hid[here, :], wq[...]).astype(BF)
-        scores = jnp.concatenate([mm_nt(queries[64 * s : 64 * s + 64], kb[4 * g + s]) for s in range(4)], axis=0) * scale
+        scores = jnp.where(same_span, mm_nt(queries, four(kb, g)) * scale, 0.0)
         raised = jnp.exp(scores)
-        probs = raised / head_sum(raised)
+        probs = jnp.where(same_span, raised / head_sum(raised), 0.0)
         prs[here, :] = probs
-        rounded = probs.astype(BF)
-        out = jnp.concatenate([mm(rounded[64 * s : 64 * s + 64], vb[4 * g + s]) for s in range(4)], axis=0)
+        out = mm(probs.astype(BF), four(vb, g))
         att[here, :] = out.astype(BF)
         att_t[:, here] = out.T.astype(BF)
         return carry
@@ -400,10 +405,10 @@
     def back(g, carry):
         here = pl.ds(pl.multiple_of(256 * g, 256), 256)
         d_att = mm(dbr[here, :], wo[...]).astype(BF)
-        d_probs = jnp.concatenate([mm_nt(d_att[64 * s : 64 * s + 64], vb[4 * g + s]) for s in range(4)], axis=0)
+        d_probs = mm_nt(d_att, four(vb, g))
         probs = prs[here, :]
         d_scores = (probs * (d_probs - head_sum(probs * d_probs))).astype(BF)
-        out = jnp.concatenate([mm(d_scores[64 * s : 64 * s + 64], kb[4 * g + s]) for s in range(4)], axis=0) * scale
+        out = mm(d_scores, four(kb, g)) * scale
         dq_t[:, here] = out.T.astype(BF)
         return carry
 
@@ -438,18 +443,28 @@
             sg[n, h, pl.ds(2 * me, 2)] = fs[n, h]
         return out
 
-    def gather(n, step, copies):
+    def gather(n, copies):
         arrive(copies)
         out = []
         for h, (me, device) in enumerate(first_of):
-            b = (me - fwd * (step - 1) + 16) % 8
-            first = sg.at[n, h, pl.ds(0, 9)]
-            out.append(go(first if step == 1 else og.at[n, h, b], og.at[n, h, b], device((me + fwd + 8) % 8)))
-            if step <= 3:
-                b = (me + fwd * (step - 1) + 16) % 8
-                out.append(go(first if step == 1 else og.at[n, h, b], og.at[n, h, b], device((me - fwd + 8) % 8)))
-            if step == 1:
-                og[n, h, me] = sg[n, h, 0:9]
+            sent = [
+                go(sg.at[n, h, pl.ds(0, 9)], og.at[n, h, me], device((me + fwd * k + 8) % 8)) for k in (2, -2, 1, -1)
+            ]
+            og[n, h, me] = sg[n, h, 0:9]
+            out.append(sent)
+        return out
+
+    def gather_on(n, before):
+        out = []
+        for h, (me, device) in enumerate(first_of):
+            ahead, behind, *near = before[h]
+            ahead.wait_recv()
+            block = og.at[n, h, (me - 2 * fwd + 8) % 8]
+            out += [go(block, block, device((me + fwd * k + 8) % 8)) for k in (2, 1)]
+            behind.wait_recv()
+            block = og.at[n, h, (me + 2 * fwd + 8) % 8]
+            out.append(go(block, block, device((me - fwd + 8) % 8)))
+            out += near
         return out
 
     def write(n, out):
@@ -463,16 +478,12 @@
     go_copies = add_up(1, go_copies)
     go_copies = finish(1, go_copies)
     gq_copies = add_up(0, gq_copies)
-    go_copies = gather(1, 1, go_copies)
+    go_copies = gather(1, go_copies)
     gq_copies = finish(0, gq_copies)
-    go_copies = gather(1, 2, go_copies)
-    gq_copies = gather(0, 1, gq_copies)
-    go_copies = gather(1, 3, go_copies)
-    gq_copies = gather(0, 2, gq_copies)
-    go_copies = gather(1, 4, go_copies)
-    gq_copies = gather(0, 3, gq_copies)
+    go_copies = gather_on(1, go_copies)
+    gq_copies = gather(0, gq_copies)
     arrive(go_copies)
-    gq_copies = gather(0, 4, gq_copies)
+    gq_copies = gather_on(0, gq_copies)
     write(1, go_out)
     arrive(gq_copies)
     write(0, gq_out)
@@ -524,7 +535,7 @@
             V((GROUP, 32, HC), BF),
             V((ROWS, H), BF),
             V((ROWS, H), BF),
-            V((ROWS, 32), F32),
+            V((ROWS, 128), F32),
             V((ROWS, HC), BF),
             V((HC, ROWS), BF),
             V((HC, ROWS), BF),

time: 131 us -> 127 us (0.969)
  the two profiles are of different devices: /device:TPU:64 before, /device:TPU:16 now
where the time goes in v5:
time: 127 us
  Pallas kernels  126 us (99%)
    pallas_call x1, Pallas kernels, body(): pl.pallas_call(kernel, out_shape=(jax.ShapeDtypeStruct((HC, H), BF), jax....  124 us
    pallas_call x1, Pallas kernels, body(): pl.pallas_call(widen, out_shape=(jax.ShapeDtypeStruct((HC, H), F32), jax....  2.74 us

profile of v5, /device:TPU:16, one launch (start us, length us, event | category | flops | bytes accessed | tf_op | source)
XLA Modules:
  0.0 127.1 jit_solution(15391653806835119504)
XLA Ops:
  0.6 123.7 %shard_map.148 = (bf16[192,1536]{1,0:T(8,128)(2,1)}, bf16[192,1536]{1,0:T(8,128)(2,1)}, f32[8,128]{1,0:T(8,128)}) custom-call(bf16[2,64,64]{2,1,0:T(8,128)(2,1)} %act.1, bf16[2,64,64]{2,1,0:T(8,128)(2,1)} %noise.1, s32[2]{0:T(128)} %emb_ids.1, s32[2]{0:T(128)} %lengths.1, s32[2]{0:T(128)} %levels.1, s32[24]{0:T(128)} %act_dims.1, bf16[128,640]{1,0:T(8,128)(2,1)} %bitcast.3, ...), custom_call_target="tpu_custom_call" | custom-call | tf_op jit(solution)/shard_map/pallas_call | solution.py:505
  124.3 2.7 %shard_map.149 = (f32[192,1536]{1,0:T(8,128)}, f32[192,1536]{1,0:T(8,128)}, f32[2]{0:T(128)}) custom-call(bf16[192,1536]{1,0:T(8,128)(2,1)} %get-tuple-element.6.q_in, bf16[192,1536]{1,0:T(8,128)(2,1)} %get-tuple-element.7.o_in, f32[8,128]{1,0:T(8,128)} %get-tuple-element.8.loss_in), custom_call_target="tpu_custom_call" | custom-call | tf_op jit(solution)/shard_map/pallas_call | solution.py:566

commit v6 on v5

--- a/solution.py
+++ b/solution.py
@@ -58,8 +58,8 @@
 def kernel(
     act, noise, emb_ids, lengths, levels, act_dims, f_in, enc_in, dec_in, wq_own, wk_own, wv_own, wo_own,
     gq_out, go_out, loss_out,
-    wa_in, wb_in, nz_in, vel_in, code_in, ids_in,
-    wa, wb, fg, eg, dg, nzg, cg, ig, ids, kv, qo, wq, wo, kb, vb,
+    wa_in, wb_in, nz_in, vel_in, freqs, ids_in,
+    wa, wb, fg, eg, dg, nzg, ig, ids, kv, qo, wq, wo, kb, vb,
     hid, dbr, prs, att, att_t, dq_t, ps, pr, dp_own, dpg,
     gs, wide, own_slice, gr, sb, sr, fs, sg, og, send_sems, recv_sems, local_sem,
 ):
@@ -95,11 +95,11 @@
     code_lane = lax.broadcasted_iota(jnp.int32, (8, 384), 1)
     half = H // 2
     freq = jnp.exp(-math.log(10000.0) * (code_lane + 384 * (code_row & 1)).astype(F32) / half)
-    level = jnp.where(code_row < 4, levels[0].astype(F32), levels[1].astype(F32))
-    angle = level * freq
-    code_in[...] = jnp.where((code_row & 2) == 0, jnp.sin(angle), jnp.cos(angle))
+    freqs[...] = freq
     id_lane = lax.broadcasted_iota(jnp.int32, (8, 128), 1)
-    ids_in[...] = jnp.where(id_lane == 0, emb_ids[0], emb_ids[1])
+    ids_in[...] = jnp.where(
+        id_lane < 2, jnp.where(id_lane == 0, emb_ids[0], emb_ids[1]), jnp.where(id_lane == 2, levels[0], levels[1])
+    )
 
     pl.semaphore_wait(barrier, (ne - 1) + (NY - 1) + (NZ - 1))
 
@@ -114,7 +114,6 @@
     for k in range(1, ne):
         peer = dev_e((j + k) % ne)
         small.append(go(nz_in, nzg.at[j], peer))
-        small.append(go(code_in, cg.at[j], peer))
         small.append(go(ids_in, ig.at[j], peer))
 
     def arrive(copies):
@@ -202,7 +201,6 @@
     eg[pl.ds(3 * j, 3)] = enc_in[...]
     dg[pl.ds(3 * j, 3)] = dec_in[...]
     nzg[j] = nz_in[...]
-    cg[j] = code_in[...]
     ig[j] = ids_in[...]
 
     ring = []
@@ -220,13 +218,28 @@
         rows = jnp.concatenate([wa[b, place_of(t, z)] for t in range(8)], axis=0)
         return mm(fg[b], rows)
 
-    def encode(p, carry):
-        enc = mm(two_spans(nzg[p]), weights_of(eg, p)).astype(BF).astype(F32)
-        code = cg[p]
-        for q in range(2):
-            row = jnp.concatenate([code[4 * q + r : 4 * q + r + 1] for r in range(4)], axis=1)
-            hid[pl.ds(pl.multiple_of(p * 128 + 64 * q, 64), 64), :] = (enc[64 * q : 64 * q + 64] + row).astype(BF)
+    def code_of(p):
+        level = jnp.where(code_row < 4, ids[p, 0, 2].astype(F32), ids[p, 0, 3].astype(F32))
+        angle = level * freqs[...]
+        return jnp.where((code_row & 2) == 0, jnp.sin(angle), jnp.cos(angle))
+
+    def encode(g, carry):
+        weights = jnp.concatenate([weights_of(eg, 2 * g), weights_of(eg, 2 * g + 1)], axis=0)
+        enc = mm(four_spans(nzg, g), weights).astype(BF).astype(F32)
+        for r in range(2):
+            code = code_of(2 * g + r)
+            for q in range(2):
+                row = jnp.concatenate([code[4 * q + t : 4 * q + t + 1] for t in range(4)], axis=1)
+                start = 128 * r + 64 * q
+                hid[pl.ds(pl.multiple_of(g * 256 + start, 64), 64), :] = (enc[start : start + 64] + row).astype(BF)
         return carry
+
+    def four_spans(buf, g):
+        upper, lower = two_spans(buf[2 * g]), two_spans(buf[2 * g + 1])
+        zero = jnp.zeros_like(upper)
+        return jnp.concatenate(
+            [jnp.concatenate([upper, zero], axis=1), jnp.concatenate([zero, lower], axis=1)], axis=0
+        )
 
     def two_spans(pair):
         zero = jnp.zeros_like(pair)
@@ -259,7 +272,7 @@
         kv[:, 0:256] += kv_part((y - fwd * step + 16) % 8) + kv_part((y + fwd * step + 16) % 8)
     ex = along_x_last(ex, e_half, e_whole)
     arrive(ex)
-    lax.fori_loop(0, ne, encode, 0)
+    lax.fori_loop(0, 4, encode, 0)
     dx = along_x_forward(dx, d_half, d_whole)
     for piece in range(3):
         for copies in ring[piece]:
@@ -373,12 +386,7 @@
     arrive(errors)
 
     def d_branch(g, carry):
-        upper, lower = two_spans(dpg[2 * g]), two_spans(dpg[2 * g + 1])
-        zero = jnp.zeros_like(upper)
-        left_rows = jnp.concatenate(
-            [jnp.concatenate([upper, zero], axis=1), jnp.concatenate([zero, lower], axis=1)], axis=0
-        )
-        dbr[pl.ds(pl.multiple_of(256 * g, 256), 256), :] = mm(left_rows, four_decoders(g)).astype(BF)
+        dbr[pl.ds(pl.multiple_of(256 * g, 256), 256), :] = mm(four_spans(dpg, g), four_decoders(g)).astype(BF)
         return carry
 
     lax.fori_loop(0, 4, d_branch, 0)
@@ -524,7 +532,6 @@
             V((EMBS, STEPS, H), BF),
             V((EMBS, STEPS, H), BF),
             V((8, STEPS, 128), BF),
-            V((8, 8, 384), F32),
             V((8, 8, 128), jnp.int32),
             pltpu.SMEM((8, 8, 128), jnp.int32),
             V((GROUP * CTX, 2 * HC), F32),

time: 127 us -> 126 us (level)
  no operation moved by 1% of the time
where the time goes in v6:
time: 126 us
  Pallas kernels  125 us (99%)
    pallas_call x1, Pallas kernels, body(): pl.pallas_call(kernel, out_shape=(jax.ShapeDtypeStruct((HC, H), BF), jax....  123 us
    pallas_call x1, Pallas kernels, body(): pl.pallas_call(widen, out_shape=(jax.ShapeDtypeStruct((HC, H), F32), jax....  2.74 us

profile of v6, /device:TPU:16, one launch (start us, length us, event | category | flops | bytes accessed | tf_op | source)
XLA Modules:
  0.0 125.9 jit_solution(7407694270130327014)
XLA Ops:
  0.6 122.5 %shard_map.148 = (bf16[192,1536]{1,0:T(8,128)(2,1)}, bf16[192,1536]{1,0:T(8,128)(2,1)}, f32[8,128]{1,0:T(8,128)}) custom-call(bf16[2,64,64]{2,1,0:T(8,128)(2,1)} %act.1, bf16[2,64,64]{2,1,0:T(8,128)(2,1)} %noise.1, s32[2]{0:T(128)} %emb_ids.1, s32[2]{0:T(128)} %lengths.1, s32[2]{0:T(128)} %levels.1, s32[24]{0:T(128)} %act_dims.1, bf16[128,640]{1,0:T(8,128)(2,1)} %bitcast.3, ...), custom_call_target="tpu_custom_call" | custom-call | tf_op jit(solution)/shard_map/pallas_call | solution.py:513
  123.2 2.7 %shard_map.149 = (f32[192,1536]{1,0:T(8,128)}, f32[192,1536]{1,0:T(8,128)}, f32[2]{0:T(128)}) custom-call(bf16[192,1536]{1,0:T(8,128)(2,1)} %get-tuple-element.6.q_in, bf16[192,1536]{1,0:T(8,128)(2,1)} %get-tuple-element.7.o_in, f32[8,128]{1,0:T(8,128)} %get-tuple-element.8.loss_in), custom_call_target="tpu_custom_call" | custom-call | tf_op jit(solution)/shard_map/pallas_call | solution.py:573
